TPU v7x, 512 devices: a whole 4x8x8 slice. The times are simulated.
512 devices in a mesh: row: 64 (over z, y), col: 8 (over x, core).
Axes of the slice: x: 4, y: 8, z: 8, core: 2. Of those that a mesh axis runs over, the one named last changes fastest.
Arguments:
- pool: float32 [131072, 128], P('row'), may hold values from -6 to 6
- window_index: int32 [16384], P('row'), may hold values from 0 to 2047
- pool_labels: int32 [131072], P('row'), may hold values from 0 to 9
- val_embed: float32 [32768, 128], P('col', 'row'), may hold values from -6 to 6
- val_labels: int32 [32768], P('col'), may hold values from 0 to 9
- class_cost: float32 [10, 10], replicated, may hold values from 0 to 1
Outputs:
- value: float32 [16384], P('row')
- potential_val: float32 [32768], P('col')
Inputs may be any that keep to these rules, and one draw needn't show every extreme that they name: `window_index`: window example i reads pool row (i // 256) * 2048 + window_index_i.
All inputs are finite; a program needn't handle non-finite values.
Results may differ from a plain program's by a relative error of at most 0.0003.
Values sent between devices are 32-bit elements; how exact they have to be, the bound alone decides.
No kernel may reach another device: no remote copies, remote signals or barrier semaphores. Data moves between devices by JAX's collectives and lax.ppermute only.
A program may use at most 64 MiB of HBM per device.

v0:
```python
import math

import jax
import jax.numpy as jnp
from jax import lax
from jax.sharding import PartitionSpec as P

ITERS = 2


EPSILON = 0.02


def merged(x, axis, combine):
    everything = jax.tree.map(lambda part: lax.all_gather(part, axis), x)
    initial = jax.tree.map(lambda part: part[0], everything)

    def lap(k, so_far):
        return combine(so_far, jax.tree.map(lambda part: part[k], everything))

    return lax.fori_loop(1, lax.axis_size(axis), lap, initial)


def cost_rows(rows, row_labels, val_t, val_onehot_t, class_cost):
    squares_r = jnp.sum(rows * rows, axis=1)
    squares_v = jnp.sum(val_t * val_t, axis=0)
    cross = jnp.dot(
        rows, val_t, precision=lax.Precision.HIGHEST, preferred_element_type=jnp.float32
    )
    onehot = (
        row_labels[:, None] == jnp.arange(class_cost.shape[0], dtype=jnp.int32)[None, :]
    ).astype(jnp.float32)
    mapped = jnp.dot(
        onehot, class_cost, precision=lax.Precision.HIGHEST, preferred_element_type=jnp.float32
    )
    label = jnp.dot(
        mapped, val_onehot_t, precision=lax.Precision.HIGHEST, preferred_element_type=jnp.float32
    )
    return (squares_r[:, None] + squares_v[None, :] - 2.0 * cross) / rows.shape[1] + label


def combine(first, second):
    top = jnp.maximum(first[0], second[0])
    return (top, first[1] * jnp.exp(first[0] - top) + second[1] * jnp.exp(second[0] - top))


def local(pool, window_index, pool_labels, val_embed, val_labels, class_cost):
    rows = jnp.take(pool, window_index, axis=0)
    row_labels = jnp.take(pool_labels, window_index, axis=0)
    val_full = lax.all_gather(val_embed, "row", axis=1, tiled=True)
    val_t = val_full.T
    classes = class_cost.shape[0]
    val_onehot_t = (jnp.arange(classes, dtype=jnp.int32)[:, None] == val_labels[None, :]).astype(
        jnp.float32
    )
    count = rows.shape[0]
    width = val_labels.shape[0]
    block = min(128, count)
    nblocks = count // block
    row_groups = lax.axis_size("row")
    total_train = count * row_groups
    log_a = -math.log(total_train)
    log_b = -math.log(width * lax.axis_size("col"))
    tiles = lax.map(
        lambda pair: cost_rows(pair[0], pair[1], val_t, val_onehot_t, class_cost),
        (rows.reshape(nblocks, block, rows.shape[1]), row_labels.reshape(nblocks, block)),
    )

    def fetch(index):
        return lax.dynamic_index_in_dim(tiles, index, 0, keepdims=False)

    indices = jnp.arange(nblocks, dtype=jnp.int32)
    potential_val = jnp.zeros((width,), jnp.float32)
    for step in range(ITERS):

        def row_stats(index):
            z = (potential_val[None, :] - fetch(index)) / EPSILON
            top = jnp.max(z, axis=1)
            return (top, jnp.sum(jnp.exp(z - top[:, None]), axis=1))

        tops, sums = lax.map(row_stats, indices)
        top, total_exp = merged((tops.reshape(count), sums.reshape(count)), "col", combine)
        f = EPSILON * log_a - EPSILON * (top + jnp.log(total_exp))
        f_blocks = f.reshape(nblocks, block)

        def exponents(index):
            return (
                lax.dynamic_index_in_dim(f_blocks, index, 0, keepdims=False)[:, None] - fetch(index)
            ) / EPSILON

        def max_step(carry, index):
            return (jnp.maximum(carry, jnp.max(exponents(index), axis=0)), None)

        local_top, unused = lax.scan(max_step, jnp.full((width,), -jnp.inf, jnp.float32), indices)
        whole_top = lax.pmax(local_top, "row")

        def sum_step(carry, index):
            return (carry + jnp.sum(jnp.exp(exponents(index) - whole_top[None, :]), axis=0), None)

        local_sum, unused = lax.scan(sum_step, jnp.zeros((width,), jnp.float32), indices)
        whole_sum = lax.psum(local_sum, "row")
        lse = whole_top + jnp.log(whole_sum)
        potential_val = EPSILON * log_b - EPSILON * lse
    whole = lax.psum(jnp.sum(f), "row")
    value = f - whole / total_train
    return (value, potential_val)


def solution(mesh):
    placed = (P("row", None), P("row"), P("row"), P("col", "row"), P("col"), P())
    return jax.shard_map(
        local, mesh=mesh, in_specs=placed, out_specs=(P("row"), P("col")), check_vma=False
    )
```

profile of v0, /device:TPU:2, one launch (start us, length us, event | category | flops | bytes accessed | tf_op | source)
XLA Modules:
  0.0 1322.0 jit_solution(9994220303686463589)
XLA Ops:
  8.7 1.9 gather_fusion.1
  11.5 88.0 %all-gather.7.cloned.1.call-done = f32[64,2,4096]{2,1,0:T(2,128)} async-done(((f32[1,2,4096]{2,1,0:T(2,128)}), f32[64,2,4096]{2,1,0:T(2,128)}) %all-gather.7.cloned.1.call-update) | async-done | bytes 2097168 | tf_op jit(solution)/shard_map/all_gather | solution.py:50
  99.5 2.7 reshape.69
  102.9 11.5 while.119
  103.0 2.1 fusion.63
  105.4 3.3 fusion.66
  108.8 2.1 fusion.63
  111.1 3.3 fusion.66
  114.4 13.0 while.115
  118.8 2.1 fusion.55
  125.3 2.1 fusion.55
  127.5 8.7 all-gather.1
  136.1 10.2 all-gather.2
  146.7 8.8 while.120
  149.2 1.9 fusion.67
  155.5 276.7 %pmax.14 = f32[4096]{0:T(1024)S(1)} all-reduce(f32[4096]{0:T(1024)S(1)} %get-tuple-element.540), channel_id=1, replica_groups=mesh['row'=64,'col'=8] {'row'}, use_global_device_ids=true, to_apply=%region_13.14 | all-reduce | flops 4096 | bytes 32768 | tf_op jit(solution)/shard_map/pmax | solution.py:95
  432.2 9.2 while.121
  434.6 2.1 fusion.68
  439.2 2.1 fusion.68
  441.4 274.0 %psum.21 = f32[4096]{0:T(1024)S(1)} all-reduce(f32[4096]{0:T(1024)S(1)} %get-tuple-element.541), channel_id=1, replica_groups=mesh['row'=64,'col'=8] {'row'}, use_global_device_ids=true, to_apply=%region_17.18 | all-reduce | flops 4096 | bytes 32768 | tf_op jit(solution)/shard_map/psum | solution.py:101
  715.4 13.1 while.117
  719.7 2.1 exponential_reduce_fusion.2
  726.2 2.1 exponential_reduce_fusion.2
  728.4 8.1 all-gather.3
  736.5 9.5 all-gather.4
  747.0 8.9 while.122
  754.0 1.9 fusion.69
  756.0 274.0 %pmax.15 = f32[4096]{0:T(1024)S(1)} all-reduce(f32[4096]{0:T(1024)S(1)} %get-tuple-element.546), channel_id=1, replica_groups=mesh['row'=64,'col'=8] {'row'}, use_global_device_ids=true, to_apply=%region_29.30 | all-reduce | flops 4096 | bytes 32768 | tf_op jit(solution)/shard_map/pmax | solution.py:95
  1029.9 9.4 while.123
  1032.5 2.1 fusion.70
  1037.2 2.1 fusion.70
  1039.3 274.0 %all-reduce = (f32[]{:T(128)}, f32[4096]{0:T(1024)S(1)}) all-reduce(f32[]{:T(128)} %get-tuple-element.760, f32[4096]{0:T(1024)S(1)} %get-tuple-element.547), channel_id=1, replica_groups=mesh['row'=64,'col'=8] {'row'}, use_global_device_ids=true, to_apply=%region_25.26 | all-reduce | flops 4097 | bytes 32776 | tf_op jit(solution)/shard_map/psum | solution.py:104
  (122 shorter events, 25.3 us)
Async XLA Ops:
  7.2 3.4 copy-start
  7.2 4.2 copy-start.2
  7.2 92.3 %all-gather.7.cloned.1.call-start = ((), (), s32[]{:S(2)}) async-start(), calls=%async_computation | async-start | bytes 2129920 | tf_op jit(solution)/shard_map/all_gather | solution.py:50
  102.2 0.7 copy-start.1
  102.2 0.7 copy-start.3
Sparse Core Ops, SparseCore 0:
  11.1 88.3 all-gather.6
where the time goes:
time: 1320 us
  blocking collectives  1130 us (86%)
  waiting for transfers between devices  88.7 us (7%)
  other arithmetic  35.3 us (3%)
  loops' own time  23.3 us (2%)
  between operations  14.9 us (1%)
  local copies, waits for them, and re-layouts  13.5 us (1%)
    pmax x2, blocking collectives, local(): whole_top = lax.pmax(local_top, 'row')  551 us
    psum x1, blocking collectives, local(): whole = lax.psum(jnp.sum(f), 'row')  274 us
    psum x1, blocking collectives, local(): whole_sum = lax.psum(local_sum, 'row')  274 us
    all_gather x1, waiting for transfers between devices, local(): val_full = lax.all_gather(val_embed, 'row', axis=1, tiled=True)  88 us
    all_gather x4, blocking collectives, merged(): everything = jax.tree.map(lambda part: lax.all_gather(part, axis), x)  36.4 us
  transfers between devices with their start and end apart: 1, of which 1 were waited for; matrix products, arithmetic and copies ran while one was open for 0% of the time, Pallas kernels for 0%

commit v1 on v0

v1 whole, which is shorter than its diff:
```python
import math

import jax
import jax.numpy as jnp
from jax import lax
from jax.experimental import pallas as pl
from jax.experimental.pallas import tpu as pltpu
from jax.sharding import Mesh
from jax.sharding import PartitionSpec as P

EPSILON = 0.02
SCALE = 1.0 / (EPSILON * math.log(2.0))
BACK = EPSILON * math.log(2.0)

ROW = ("z2", "z1", "z0", "y2", "y1", "y0")
COL = ("x", "core")
QUAD = ("z0", "y0")
ACROSS = ("z2", "z1", "y2", "y1")
ALONG = QUAD + COL

T = 128
NB = 8
SIDE = NB * T
PARAMS = pltpu.CompilerParams(vmem_limit_bytes=48 * 1024 * 1024)
F32 = jnp.float32
BF16 = jnp.bfloat16


def split3(x):
    hi = x.astype(BF16)
    rest = x - hi.astype(F32)
    mid = rest.astype(BF16)
    low = (rest - mid.astype(F32)).astype(BF16)
    return hi, mid, low


def lse_lead(parts):
    top = jnp.max(parts, axis=0)
    return top + jnp.log2(jnp.sum(jnp.exp2(parts - top[None]), axis=0))


def lse_list(zs):
    top = zs[0]
    for z in zs[1:]:
        top = jnp.maximum(top, z)
    total = jnp.exp2(zs[0] - top)
    for z in zs[1:]:
        total = total + jnp.exp2(z - top)
    return top, total


def columns_kernel(val_ref, out_ref):
    for quarter in range(4):
        for block in range(NB):
            piece = val_ref[:, pl.ds((quarter * NB + block) * T, T)]
            for feature in range(2):
                row = piece[feature : feature + 1]
                for z in range(4):
                    for y in range(4):
                        target = ((z * 2 + quarter // 2) * 4 + y) * 2 + quarter % 2
                        out_ref[target, pl.ds(feature * NB + block, 1), :] = row


def rows_kernel(index_ref, labels_ref, pool_ref, out_ref, column_ref):
    count = index_ref.shape[0]

    def step(i, carry):
        for j in range(8):
            at = i * 8 + j
            place = index_ref[at]
            out_ref[0, pl.ds(at, 1), :] = pool_ref[pl.ds(place, 1), :]
            column_ref[pl.ds(at, 1), :] = jnp.full((1, T), labels_ref[place].astype(F32), F32)
        return carry

    lax.fori_loop(0, count // 8, step, 0)
    out_ref[0, count : count + 8, :] = jnp.zeros((8, T), F32)
    for k in range(count // T):
        flat = column_ref[k * T : (k + 1) * T, :].T
        out_ref[0, count + k : count + k + 1, :] = flat[0:1]
    for copy in range(1, 4):
        out_ref[copy] = out_ref[0]


def row_lse(load, at_ref, out_ref):
    def block_step(s, carry):
        for piece in range(T // 32):
            rows = pl.ds(s * T + piece * 32, 32)
            top, total = lse_list([load(block, rows) for block in range(NB)])
            at_ref[piece * 32 : (piece + 1) * 32, :] = top + jnp.log2(total)
        flat = at_ref[...].T
        top = jnp.max(flat, axis=0, keepdims=True)
        lse = top + jnp.log2(jnp.sum(jnp.exp2(flat - top), axis=0, keepdims=True))
        out_ref[pl.ds(s, 1), :] = lse
        return carry

    lax.fori_loop(0, NB, block_step, 0)


def cost_kernel(rows_ref, val_ref, quarter_ref, labels_ref, class_ref, cost_ref, out_ref, b_ref, sq_ref, at_ref, part_ref):
    count = 256
    classes = class_ref.shape[0]
    own = labels_ref[pl.ds(pl.multiple_of(quarter_ref[0] * NB, NB), NB), :]
    kinds = class_ref[...] * (-SCALE)
    for block in range(NB):
        lanes = slice(block * T, (block + 1) * T)
        y = val_ref[pl.ds(block, T, stride=NB), :]
        hi, mid, low = split3(y)
        for k, part in enumerate((hi, mid, hi, low, hi, mid)):
            b_ref[k * T : (k + 1) * T, lanes] = part
        sq_ref[0:1, lanes] = jnp.sum(y * y, axis=0, keepdims=True) * (-SCALE / T)
        onehot = (lax.broadcasted_iota(jnp.int32, (classes, T), 0) == own[block : block + 1]).astype(F32)
        mapped = jnp.dot(kinds, onehot, precision=lax.Precision.HIGHEST, preferred_element_type=F32)
        mapped = jnp.concatenate([mapped, jnp.zeros((16 - classes, T), F32)], axis=0)
        hi, mid, low = split3(mapped)
        b_ref[6 * T : 7 * T, lanes] = jnp.concatenate([hi, mid, low, jnp.zeros((T - 48, T), BF16)], axis=0)
    for group in range(4):
        x = rows_ref[group, 0:count, :]
        squares = jnp.sum(x * x, axis=1, keepdims=True) * (-SCALE / T)
        hi, mid, low = split3(x * (2.0 * SCALE / T))
        lane = lax.broadcasted_iota(jnp.int32, (count, T), 1)
        flat = [
            jnp.broadcast_to(rows_ref[group, count + k : count + k + 1, :], (T, T)).T for k in range(count // T)
        ]
        label = jnp.concatenate(flat, axis=0).astype(jnp.int32)
        ext = jnp.where((lane % 16 == label) & (lane < 48), 1.0, 0.0).astype(BF16)
        a = jnp.concatenate([hi, hi, mid, hi, low, mid, ext], axis=1)
        product = jnp.dot(a, b_ref[...], preferred_element_type=F32)
        cost_ref[group * count : (group + 1) * count, :] = product + squares + sq_ref[0:1, :]
    row_lse(lambda block, rows: cost_ref[rows, block * T : (block + 1) * T], at_ref, part_ref)
    for k in range(out_ref.shape[0]):
        out_ref[k] = part_ref[...]


def rows_step_kernel(parts_ref, cost_ref, out_ref, at_ref, part_ref):
    g = -15.0 - lse_lead(parts_ref[...])
    wide = [jnp.broadcast_to(g[block : block + 1], (32, T)) for block in range(NB)]
    row_lse(lambda block, rows: cost_ref[rows, block * T : (block + 1) * T] + wide[block], at_ref, part_ref)
    for k in range(out_ref.shape[0]):
        out_ref[k] = part_ref[...]


def column_lse(f, cost_ref, wide_ref, part_ref):
    for s in range(NB):
        wide_ref[s * T : (s + 1) * T, :] = jnp.broadcast_to(f[s : s + 1], (T, T)).T
    for block in range(NB):
        lanes = slice(block * T, (block + 1) * T)

        def chunk(k, carry):
            start = pl.multiple_of(k * 64, 64)
            zs = [
                cost_ref[pl.ds(start + 8 * j, 8), lanes] + wide_ref[pl.ds(start + 8 * j, 8), :]
                for j in range(8)
            ]
            top, total = lse_list(zs)
            newtop = jnp.maximum(carry[0], top)
            return newtop, carry[1] * jnp.exp2(carry[0] - newtop) + total * jnp.exp2(top - newtop)

        start = (jnp.full((8, T), -3.0e38, F32), jnp.zeros((8, T), F32))
        top, total = lax.fori_loop(0, SIDE // 64, chunk, start, unroll=4)
        best = jnp.max(top, axis=0, keepdims=True)
        whole = jnp.sum(total * jnp.exp2(top - best), axis=0, keepdims=True)
        part_ref[block : block + 1, :] = best + jnp.log2(whole)


def columns_step_kernel(parts_ref, cost_ref, out_ref, wide_ref, part_ref):
    f = -14.0 - lse_lead(parts_ref[...])
    column_lse(f, cost_ref, wide_ref, part_ref)
    for k in range(out_ref.shape[0]):
        out_ref[k] = part_ref[...]


def last_columns_kernel(parts_ref, cost_ref, out_ref, f_ref, wide_ref, part_ref):
    f = -14.0 - lse_lead(parts_ref[...])
    f_ref[...] = f
    column_lse(f, cost_ref, wide_ref, part_ref)
    total = jnp.broadcast_to(jnp.sum(f, axis=0, keepdims=True), (NB, T))
    for k in range(out_ref.shape[0]):
        out_ref[k, 0:NB, :] = part_ref[...]
        out_ref[k, NB : 2 * NB, :] = total


def finish_kernel(parts_ref, f_ref, quarter_ref, value_ref, potential_ref):
    total = jnp.zeros((NB, T), F32)
    for k in range(parts_ref.shape[0]):
        total = total + parts_ref[k, NB : 2 * NB, :]
    mean = jnp.sum(total[0:1]) * (0.25 / 16384.0)
    value_ref[...] = (f_ref[pl.ds(quarter_ref[0] * 2, 2), :] - mean) * BACK
    for quarter in range(4):
        parts = [
            parts_ref[((z * 2 + quarter // 2) * 4 + y) * 2 + quarter % 2, 0:NB, :] for z in range(4) for y in range(4)
        ]
        top, whole = lse_list(parts)
        potential_ref[quarter * NB : (quarter + 1) * NB, :] = (-15.0 - (top + jnp.log2(whole))) * BACK


def vmem(shape, dtype=F32):
    return pltpu.VMEM(shape, dtype)


SPEC = pl.BlockSpec(memory_space=pltpu.VMEM)
SCALARS = pl.BlockSpec(memory_space=pltpu.SMEM)


def call(kernel, out, ins, scratch=()):
    def shape(s):
        return jax.ShapeDtypeStruct(s, F32)

    return pl.pallas_call(
        kernel,
        out_shape=[shape(s) for s in out],
        in_specs=[SCALARS if i else SPEC for i in ins],
        out_specs=[SPEC] * len(out),
        scratch_shapes=list(scratch),
        compiler_params=PARAMS,
    )


def local(pool, window_index, pool_labels, val_embed, val_labels, class_cost):
    quarter = lax.axis_index(QUAD).astype(jnp.int32).reshape(1)
    (columns,) = call(columns_kernel, [(64, 16, T)], [0])(val_embed.T)
    (rows,) = call(rows_kernel, [(4, 264, T)], [1, 1, 0], [vmem((256, T))])(window_index, pool_labels, pool)
    columns = lax.all_to_all(columns, ROW, 0, 0)
    rows = lax.all_to_all(rows, QUAD, 0, 0)
    flat, wide = vmem((T, T)), vmem((SIDE, T))
    part = vmem((NB, T))
    cost, parts = call(
        cost_kernel,
        [(SIDE, SIDE), (32, NB, T)],
        [0, 0, 1, 0, 0],
        [vmem((7 * T, SIDE), BF16), vmem((8, SIDE)), flat, part],
    )(rows, columns.reshape(SIDE, T), quarter, val_labels.reshape(32, T), class_cost)
    parts = lax.all_to_all(parts, ALONG, 0, 0)
    (parts,) = call(columns_step_kernel, [(16, NB, T)], [0, 0], [wide, part])(parts, cost)
    parts = lax.all_to_all(parts, ACROSS, 0, 0)
    (parts,) = call(rows_step_kernel, [(32, NB, T)], [0, 0], [flat, part])(parts, cost)
    parts = lax.all_to_all(parts, ALONG, 0, 0)
    parts, f = call(last_columns_kernel, [(64, 2 * NB, T), (NB, T)], [0, 0], [wide, part])(parts, cost)
    parts = lax.all_to_all(parts, ROW, 0, 0)
    value, potential = call(finish_kernel, [(2, T), (32, T)], [0, 0, 1])(parts, f, quarter)
    return value.reshape(256), potential.reshape(4096)


def solution(mesh):
    fine = Mesh(mesh.devices.reshape(2, 2, 2, 2, 2, 2, 4, 2), ROW + COL)
    placed = (P(ROW, None), P(ROW), P(ROW), P(COL, ROW), P(COL), P())
    return jax.shard_map(local, mesh=fine, in_specs=placed, out_specs=(P(ROW), P(COL)), check_vma=False)
```

time: 1320 us -> 128 us (0.10)
  the two profiles are of different devices: /device:TPU:2 before, /device:TPU:8 now
where the time goes in v1:
time: 128 us; the launch traced here: 127 us
  blocking collectives  63.7 us (50%)
  waiting for transfers between devices  22.8 us (18%)
  starting transfers between devices  22.4 us (18%)
  Pallas kernels  14.5 us (11%)
  local copies, waits for them, and re-layouts  3.36 us (3%)
    all_to_all x1, blocking collectives, local(): parts = lax.all_to_all(parts, ROW, 0, 0)  24.5 us
    all_to_all x2, blocking collectives, local(): parts = lax.all_to_all(parts, ALONG, 0, 0)  22.1 us
    all_to_all x1, waiting for transfers between devices, local(): columns = lax.all_to_all(columns, ROW, 0, 0)  18.6 us
    all_to_all x1, blocking collectives, local(): parts = lax.all_to_all(parts, ACROSS, 0, 0)  17.1 us
    all_to_all x1, starting transfers between devices, local(): columns = lax.all_to_all(columns, ROW, 0, 0)  13.1 us
    all_to_all x1, starting transfers between devices, local(): rows = lax.all_to_all(rows, QUAD, 0, 0)  9.26 us
    pallas_call x1, Pallas kernels, local(): call(cost_kernel, [(SIDE, SIDE), (32, NB, T)], [0, 0, 1, 0, 0], [vmem((7...  4.42 us
    all_to_all x1, waiting for transfers between devices, local(): rows = lax.all_to_all(rows, QUAD, 0, 0)  4.16 us
  transfers between devices with their start and end apart: 2, of which 2 were waited for; matrix products, arithmetic and copies ran while one was open for 0% of the time, Pallas kernels for 1%

profile of v1, /device:TPU:8, one launch (start us, length us, event | category | flops | bytes accessed | tf_op | source)
XLA Modules:
  0.0 127.4 jit_solution(18280837457071398985)
XLA Ops:
  0.6 0.0 copy-start
  0.6 1.2 copy-done
  1.9 0.0 copy-start.3
  1.9 0.7 copy-done.3
  2.6 0.0 copy-start.5
  2.6 0.7 copy-done.5
  3.2 0.0 copy-start.2
  3.2 0.0 copy-start.4
  3.2 2.1 %shard_map.77 = f32[4,264,128]{2,1,0:T(8,128)} custom-call(s32[256]{0:T(256)S(1)} %copy-done.5, s32[2048]{0:T(1024)S(1)} %copy-done.3, f32[2048,128]{1,0:T(8,128)S(1)} %copy-done), custom_call_target="tpu_custom_call" | custom-call | tf_op jit(solution)/shard_map/pallas_call | solution.py:221
  5.4 9.3 %all-to-all-start = ((f32[4,264,128]{2,1,0:T(8,128)}), f32[4,264,128]{2,1,0:T(8,128)S(1)}, u32[]{:S(2)}, u32[]{:S(2)}) async-start(f32[4,264,128]{2,1,0:T(8,128)} %shard_map.77), calls=%async_computation | async-start | bytes 1081344 | tf_op jit(solution)/shard_map/all_to_all | solution.py:223
  14.6 0.0 copy-start.1
  14.6 0.8 copy-done.1
  15.4 1.2 shard_map.78
  16.6 4.2 %all-to-all-done.rows_ref = f32[4,264,128]{2,1,0:T(8,128)S(1)} async-done(((f32[4,264,128]{2,1,0:T(8,128)}), f32[4,264,128]{2,1,0:T(8,128)S(1)}, u32[]{:S(2)}, u32[]{:S(2)}) %all-to-all-start) | async-done | bytes 540704 | tf_op jit(solution)/shard_map/all_to_all | solution.py:223
  20.7 13.1 %all-to-all-start.1 = ((f32[64,16,128]{2,1,0:T(8,128)}), f32[64,16,128]{2,1,0:T(8,128)S(1)}, u32[]{:S(2)}, u32[]{:S(2)}) async-start(f32[64,16,128]{2,1,0:T(8,128)} %shard_map.78), calls=%async_computation.1 | async-start | bytes 1048576 | tf_op jit(solution)/shard_map/all_to_all | solution.py:222
  33.9 18.6 %all-to-all-done.1 = f32[64,16,128]{2,1,0:T(8,128)S(1)} async-done(((f32[64,16,128]{2,1,0:T(8,128)}), f32[64,16,128]{2,1,0:T(8,128)S(1)}, u32[]{:S(2)}, u32[]{:S(2)}) %all-to-all-start.1) | async-done | bytes 524320 | tf_op jit(solution)/shard_map/all_to_all | solution.py:222
  52.5 0.0 copy-done.2
  52.5 0.0 copy-done.4
  52.5 4.4 %shard_map.79 = (f32[1024,1024]{1,0:T(8,128)S(1)}, f32[32,8,128]{2,1,0:T(8,128)S(1)}) custom-call(f32[4,264,128]{2,1,0:T(8,128)S(1)} %all-to-all-done.rows_ref, f32[1024,128]{1,0:T(8,128)S(1)} %bitcast.6, s32[1]{0:T(128)} %bitcast.2.quarter_ref, s32[32,128]{1,0:T(8,128)S(1)} %bitcast.8, f32[10,10]{1,0:T(8,128)S(1)} %copy-done.4), custom_call_target="tpu_custom_call" | custom-call | tf_op jit(solution)/shard_map/pallas_call | solution.py:226
  56.9 11.9 %all_to_all.30.parts_ref = f32[32,8,128]{2,1,0:T(8,128)S(1)} all-to-all(f32[32,8,128]{2,1,0:T(8,128)S(1)} %get-tuple-element.8), channel_id=1, replica_groups=mesh['z2'=2,'z1'=2,'z0'=2,'y2'=2,'y1'=2,'y0'=2,'x'=4,'core'=2] {'z0','y0..., dimensions={0} | all-to-all | bytes 262144 | tf_op jit(solution)/shard_map/all_to_all | solution.py:232
  68.8 2.1 %shard_map.80 = f32[16,8,128]{2,1,0:T(8,128)S(1)} custom-call(f32[32,8,128]{2,1,0:T(8,128)S(1)} %all_to_all.30.parts_ref, f32[1024,1024]{1,0:T(8,128)S(1)} %get-tuple-element.9.cost_ref), custom_call_target="tpu_custom_call" | custom-call | tf_op jit(solution)/shard_map/pallas_call | solution.py:233
  70.9 17.1 %all_to_all.31.parts_ref = f32[16,8,128]{2,1,0:T(8,128)S(1)} all-to-all(f32[16,8,128]{2,1,0:T(8,128)S(1)} %shard_map.80), channel_id=1, replica_groups=mesh['z2'=2,'z1'=2,'z0'=2,'y2'=2,'y1'=2,'y0'=2,'x'=4,'core'=2] {'z2','z1..., dimensions={0} | all-to-all | bytes 131072 | tf_op jit(solution)/shard_map/all_to_all | solution.py:234
  88.1 1.8 %shard_map.81 = f32[32,8,128]{2,1,0:T(8,128)S(1)} custom-call(f32[16,8,128]{2,1,0:T(8,128)S(1)} %all_to_all.31.parts_ref, f32[1024,1024]{1,0:T(8,128)S(1)} %get-tuple-element.9.cost_ref), custom_call_target="tpu_custom_call" | custom-call | tf_op jit(solution)/shard_map/pallas_call | solution.py:235
  89.9 10.2 %all_to_all.32.parts_ref = f32[32,8,128]{2,1,0:T(8,128)S(1)} all-to-all(f32[32,8,128]{2,1,0:T(8,128)S(1)} %shard_map.81), channel_id=1, replica_groups=mesh['z2'=2,'z1'=2,'z0'=2,'y2'=2,'y1'=2,'y0'=2,'x'=4,'core'=2] {'z0','y0..., dimensions={0} | all-to-all | bytes 262144 | tf_op jit(solution)/shard_map/all_to_all | solution.py:236
  100.0 2.1 %shard_map.82 = (f32[64,16,128]{2,1,0:T(8,128)S(1)}, f32[8,128]{1,0:T(8,128)S(1)}) custom-call(f32[32,8,128]{2,1,0:T(8,128)S(1)} %all_to_all.32.parts_ref, f32[1024,1024]{1,0:T(8,128)S(1)} %get-tuple-element.9.cost_ref), custom_call_target="tpu_custom_call" | custom-call | tf_op jit(solution)/shard_map/pallas_call | solution.py:237
  102.2 24.5 %all_to_all.33.parts_ref = f32[64,16,128]{2,1,0:T(8,128)S(1)} all-to-all(f32[64,16,128]{2,1,0:T(8,128)S(1)} %get-tuple-element.10), channel_id=1, replica_groups=mesh['z2'=2,'z1'=2,'z0'=2,'y2'=2,'y1'=2,'y0'=2,'x'=4,'core'=2] {'z2','z1..., dimensions={0} | all-to-all | bytes 1048576 | tf_op jit(solution)/shard_map/all_to_all | solution.py:238
  126.7 0.7 shard_map.83
Async XLA Ops:
  0.6 1.2 copy-start
  1.9 0.7 copy-start.3
  2.6 0.7 copy-start.5
  3.2 49.3 %copy-start.2 = (s32[4096]{0:T(1024)S(1)}, s32[4096]{0:T(1024)}, u32[]{:S(2)}) copy-start(s32[4096]{0:T(1024)} %param.10) | copy-start | bytes 49156
  3.2 49.3 %copy-start.4 = (f32[10,10]{1,0:T(8,128)S(1)}, f32[10,10]{1,0:T(8,128)}, u32[]{:S(2)}) copy-start(f32[10,10]{1,0:T(8,128)} %class_ref.1) | copy-start | bytes 1204
  5.4 15.4 %all-to-all-start = ((f32[4,264,128]{2,1,0:T(8,128)}), f32[4,264,128]{2,1,0:T(8,128)S(1)}, u32[]{:S(2)}, u32[]{:S(2)}) async-start(f32[4,264,128]{2,1,0:T(8,128)} %shard_map.77), calls=%async_computation | async-start | bytes 1081344 | tf_op jit(solution)/shard_map/all_to_all | solution.py:223
  14.6 0.8 copy-start.1
  20.7 31.8 %all-to-all-start.1 = ((f32[64,16,128]{2,1,0:T(8,128)}), f32[64,16,128]{2,1,0:T(8,128)S(1)}, u32[]{:S(2)}, u32[]{:S(2)}) async-start(f32[64,16,128]{2,1,0:T(8,128)} %shard_map.78), calls=%async_computation.1 | async-start | bytes 1048576 | tf_op jit(solution)/shard_map/all_to_all | solution.py:222

commit v2 on v1

v2 whole, which is shorter than its diff:
```python
import math

import jax
import jax.numpy as jnp
from jax import lax
from jax.experimental import pallas as pl
from jax.experimental.pallas import tpu as pltpu
from jax.sharding import Mesh
from jax.sharding import PartitionSpec as P

EPSILON = 0.02
SCALE = 1.0 / (EPSILON * math.log(2.0))
BACK = EPSILON * math.log(2.0)

ROW = ("z2", "z1", "z0", "y2", "y1", "y0")
COL = ("x", "core")
QUAD = ("z0", "y0")
ACROSS = ("z2", "z1", "y2", "y1")
ALONG = QUAD + COL

T = 128
NB = 8
SIDE = NB * T
OWN = 256
PARAMS = pltpu.CompilerParams(vmem_limit_bytes=20 * 1024 * 1024)
F32 = jnp.float32
BF16 = jnp.bfloat16


def split3(x):
    hi = x.astype(BF16)
    rest = x - hi.astype(F32)
    mid = rest.astype(BF16)
    low = (rest - mid.astype(F32)).astype(BF16)
    return hi, mid, low


def member(quarter, z, y):
    return ((z * 2 + quarter // 2) * 4 + y) * 2 + quarter % 2


def tree(op, xs):
    xs = list(xs)
    while len(xs) > 1:
        xs = [op(*xs[i : i + 2]) if i + 1 < len(xs) else xs[i] for i in range(0, len(xs), 2)]
    return xs[0]


def lse_list(zs):
    top = tree(jnp.maximum, zs)
    return top, tree(jnp.add, [jnp.exp2(z - top) for z in zs])


def lse_lead(parts_ref):
    top, total = lse_list([parts_ref[k] for k in range(parts_ref.shape[0])])
    return top + jnp.log2(total)


def send(part_ref, out_ref):
    part = part_ref[...]
    for k in range(out_ref.shape[0]):
        out_ref[k] = part


def prepare_kernel(
    index_hbm, labels_hbm, pool_hbm, val_hbm, columns_ref, rows_ref, index_ref, labels_ref, pool_ref, val_ref, column_ref, sems
):
    moves = [(val_hbm, val_ref), (index_hbm, index_ref), (labels_hbm, labels_ref), (pool_hbm, pool_ref)]
    copies = [pltpu.make_async_copy(a, b, sems.at[k]) for k, (a, b) in enumerate(moves)]
    for copy in copies:
        copy.start()
    copies[0].wait()
    for quarter in range(4):
        first = member(quarter, 0, 0)
        for block in range(NB):
            piece = val_ref[:, pl.ds((quarter * NB + block) * T, T)]
            for feature in range(2):
                columns_ref[first, pl.ds(feature * NB + block, 1), :] = piece[feature : feature + 1]
        whole = columns_ref[first]
        for z in range(4):
            for y in range(4):
                if z or y:
                    columns_ref[member(quarter, z, y)] = whole
    for copy in copies[1:]:
        copy.wait()

    def step(i, carry):
        for j in range(16):
            at = i * 16 + j
            place = index_ref[at]
            rows_ref[pl.ds(at, 1), :] = pool_ref[pl.ds(place, 1), :]
            column_ref[pl.ds(at, 1), :] = jnp.full((1, T), labels_ref[place].astype(F32), F32)
        return carry

    lax.fori_loop(0, OWN // 16, step, 0)
    flat = [column_ref[k * T : (k + 1) * T, :].T[0:1] for k in range(OWN // T)]
    rows_ref[OWN : OWN + 8, :] = jnp.concatenate(flat + [jnp.zeros((8 - OWN // T, T), F32)], axis=0)


def labels_kernel(quarter_ref, labels_ref, class_ref, out_ref):
    classes = class_ref.shape[0]
    own = labels_ref[pl.ds(pl.multiple_of(quarter_ref[0] * NB, NB), NB), :]
    kinds = class_ref[...] * (-SCALE)
    for block in range(NB):
        onehot = (lax.broadcasted_iota(jnp.int32, (classes, T), 0) == own[block : block + 1]).astype(F32)
        mapped = jnp.dot(kinds, onehot, precision=lax.Precision.HIGHEST, preferred_element_type=F32)
        mapped = jnp.concatenate([mapped, jnp.zeros((16 - classes, T), F32)], axis=0)
        hi, mid, low = split3(mapped)
        filled = jnp.concatenate([hi, mid, low, jnp.zeros((T - 48, T), BF16)], axis=0)
        out_ref[:, block * T : (block + 1) * T] = filled


def rows_block(load, piece_ref):
    for piece in range(T // 32):
        top, total = lse_list([load(block, piece * 32) for block in range(NB)])
        piece_ref[piece * 32 : (piece + 1) * 32, :] = top + jnp.log2(total)
    flat = piece_ref[...].T
    top = jnp.max(flat, axis=0, keepdims=True)
    return top + jnp.log2(jnp.sum(jnp.exp2(flat - top), axis=0, keepdims=True))


def group_costs(rows_ref, group, b, squares_v, cost_ref, part_ref, piece_ref):
    x = rows_ref[0:OWN, :]
    squares = jnp.sum(x * x, axis=1, keepdims=True) * (-SCALE / T)
    hi, mid, low = split3(x * (2.0 * SCALE / T))
    lane = lax.broadcasted_iota(jnp.int32, (OWN, T), 1)
    flat = [jnp.broadcast_to(rows_ref[OWN + k : OWN + k + 1, :], (T, T)).T for k in range(OWN // T)]
    label = jnp.concatenate(flat, axis=0).astype(jnp.int32)
    ext = jnp.where((lane % 16 == label) & (lane < 48), 1.0, 0.0).astype(BF16)
    a = jnp.concatenate([hi, hi, mid, hi, low, mid, ext], axis=1)
    start = pl.multiple_of(group * OWN, OWN)
    cost_ref[pl.ds(start, OWN), :] = jnp.dot(a, b, preferred_element_type=F32) + squares + squares_v
    for half in range(OWN // T):

        def load(block, row):
            return cost_ref[pl.ds(start + half * T + row, 32), block * T : (block + 1) * T]

        part_ref[pl.ds(group * 2 + half, 1), :] = rows_block(load, piece_ref.at[half])


def own_costs_kernel(rows_ref, val_ref, kinds_ref, cost_ref, part_ref, b_ref, squares_ref, piece_ref):
    for block in range(NB):
        lanes = slice(block * T, (block + 1) * T)
        y = val_ref[pl.ds(block, T, stride=NB), :]
        hi, mid, low = split3(y)
        for k, part in enumerate((hi, mid, hi, low, hi, mid)):
            b_ref[k * T : (k + 1) * T, lanes] = part
        squares_ref[:, lanes] = jnp.broadcast_to(jnp.sum(y * y, axis=0, keepdims=True) * (-SCALE / T), (8, T))
    b_ref[6 * T : 7 * T, :] = kinds_ref[...]
    group_costs(rows_ref, 0, b_ref[...], squares_ref[0:1, :], cost_ref, part_ref, piece_ref)


def other_costs_kernel(
    rows1_ref, rows2_ref, rows3_ref, b_ref, squares_ref, quarter_ref, own_ref, part_ref, cost_ref, out_ref, full_ref, piece_ref
):
    quarter = quarter_ref[0]
    full_ref[pl.ds(quarter * 2, 2), :] = part_ref[0:2, :]
    cost_ref[pl.ds(pl.multiple_of(quarter * OWN, OWN), OWN), :] = own_ref[...]
    for apart, rows_ref in enumerate((rows1_ref, rows2_ref, rows3_ref)):
        group = quarter ^ (apart + 1)
        group_costs(rows_ref, group, b_ref[...], squares_ref[0:1, :], cost_ref, full_ref, piece_ref.at[apart])
    send(full_ref, out_ref)


def rows_step_kernel(parts_ref, cost_ref, out_ref, piece_ref, part_ref):
    g = -15.0 - lse_lead(parts_ref)
    wide = [jnp.broadcast_to(g[block : block + 1], (32, T)) for block in range(NB)]
    for s in range(NB):

        def load(block, row):
            return cost_ref[s * T + row : s * T + row + 32, block * T : (block + 1) * T] + wide[block]

        part_ref[s : s + 1, :] = rows_block(load, piece_ref.at[s])
    send(part_ref, out_ref)


def columns_lse(f, cost_ref, wide_ref, part_ref):
    for s in range(NB):
        wide_ref[s * T : (s + 1) * T, :] = jnp.broadcast_to(f[s : s + 1], (T, T)).T
    for block in range(NB):
        lanes = slice(block * T, (block + 1) * T)
        tops, totals = [], []
        for start in range(0, SIDE, 64):
            rows = [slice(start + 8 * j, start + 8 * j + 8) for j in range(8)]
            top, total = lse_list([cost_ref[r, lanes] + wide_ref[r, :] for r in rows])
            tops.append(top)
            totals.append(total)
        best = jnp.max(tree(jnp.maximum, tops), axis=0, keepdims=True)
        total = tree(jnp.add, [total * jnp.exp2(top - best) for top, total in zip(tops, totals)])
        part_ref[block : block + 1, :] = best + jnp.log2(jnp.sum(total, axis=0, keepdims=True))


def columns_step_kernel(parts_ref, cost_ref, out_ref, wide_ref, part_ref):
    f = -14.0 - lse_lead(parts_ref)
    columns_lse(f, cost_ref, wide_ref, part_ref)
    send(part_ref, out_ref)


def last_columns_kernel(parts_ref, cost_ref, out_ref, f_ref, wide_ref, part_ref, row_ref):
    f = -14.0 - lse_lead(parts_ref)
    f_ref[...] = f
    columns_lse(f, cost_ref, wide_ref, part_ref)
    for block in range(NB):
        row_ref[:, block * T : (block + 1) * T] = part_ref[block : block + 1, :]
    row_ref[:, SIDE : SIDE + T] = jnp.sum(f, axis=0, keepdims=True)
    send(row_ref, out_ref)


def finish_kernel(parts_ref, f_ref, quarter_ref, value_ref, potential_ref):
    total = tree(jnp.add, [parts_ref[k, :, SIDE : SIDE + T] for k in range(parts_ref.shape[0])])
    mean = jnp.sum(total) * (0.25 / 16384.0)
    value_ref[...] = (f_ref[pl.ds(quarter_ref[0] * 2, 2), :] - mean) * BACK
    for quarter in range(4):
        parts = [parts_ref[member(quarter, z, y), :, 0:SIDE] for z in range(4) for y in range(4)]
        top, whole = lse_list(parts)
        potential_ref[quarter] = (-15.0 - (top + jnp.log2(whole))) * BACK


SPEC = pl.BlockSpec(memory_space=pltpu.VMEM)
SCALARS = pl.BlockSpec(memory_space=pltpu.SMEM)
FAR = pl.BlockSpec(memory_space=pltpu.HBM)


def vmem(shape, dtype=F32):
    return pltpu.VMEM(shape, dtype)


def shape(dims, dtype=F32):
    return jax.ShapeDtypeStruct(dims, dtype)


def call(kernel, out, ins, scratch=()):
    return pl.pallas_call(
        kernel,
        out_shape=out,
        in_specs=ins,
        out_specs=[SPEC] * len(out),
        scratch_shapes=list(scratch),
        compiler_params=PARAMS,
    )


def local(pool, window_index, pool_labels, val_embed, val_labels, class_cost):
    quarter = lax.axis_index(QUAD).astype(jnp.int32).reshape(1)
    columns, rows = call(
        prepare_kernel,
        [shape((64, 16, T)), shape((OWN + 8, T))],
        [FAR] * 4,
        [
            pltpu.SMEM(window_index.shape, jnp.int32),
            pltpu.SMEM(pool_labels.shape, jnp.int32),
            vmem(pool.shape),
            vmem((2, 4096)),
            vmem((OWN, T)),
            pltpu.SemaphoreType.DMA((4,)),
        ],
    )(*[pltpu.with_memory_space_constraint(x, pltpu.HBM) for x in (window_index, pool_labels, pool, val_embed.T)])
    columns = lax.all_to_all(columns, ROW, 0, 0)
    others = [lax.ppermute(rows, QUAD, [(i, i ^ apart) for i in range(4)]) for apart in (1, 2, 3)]
    rows, val_labels, class_cost = lax.optimization_barrier((rows, val_labels, class_cost))
    (kinds,) = call(labels_kernel, [shape((T, SIDE), BF16)], [SCALARS, SPEC, SPEC])(
        quarter, val_labels.reshape(32, T), class_cost
    )
    part, piece, wide = vmem((NB, T)), vmem((NB, T, T)), vmem((SIDE, T))
    own, part_own, b, squares = call(
        own_costs_kernel,
        [shape((OWN, SIDE)), shape((NB, T)), shape((7 * T, SIDE), BF16), shape((8, SIDE))],
        [SPEC] * 3,
        [vmem((2, T, T))],
    )(rows, columns.reshape(SIDE, T), kinds)
    cost, parts = call(
        other_costs_kernel,
        [shape((SIDE, SIDE)), shape((32, NB, T))],
        [SPEC] * 5 + [SCALARS] + [SPEC] * 2,
        [part, vmem((3, 2, T, T))],
    )(*others, b, squares, quarter, own, part_own)
    parts = lax.all_to_all(parts, ALONG, 0, 0)
    (parts,) = call(columns_step_kernel, [shape((16, NB, T))], [SPEC] * 2, [wide, part])(parts, cost)
    parts = lax.all_to_all(parts, ACROSS, 0, 0)
    (parts,) = call(rows_step_kernel, [shape((32, NB, T))], [SPEC] * 2, [piece, part])(parts, cost)
    parts = lax.all_to_all(parts, ALONG, 0, 0)
    parts, f = call(
        last_columns_kernel, [shape((64, 1, SIDE + T)), shape((NB, T))], [SPEC] * 2, [wide, part, vmem((1, SIDE + T))]
    )(parts, cost)
    parts = lax.all_to_all(parts, ROW, 0, 0)
    value, potential = call(finish_kernel, [shape((2, T)), shape((4, 1, SIDE))], [SPEC, SPEC, SCALARS])(parts, f, quarter)
    return value.reshape(256), potential.reshape(4096)


def solution(mesh):
    fine = Mesh(mesh.devices.reshape(2, 2, 2, 2, 2, 2, 4, 2), ROW + COL)
    placed = (P(ROW, None), P(ROW), P(ROW), P(COL, ROW), P(COL), P())
    return jax.shard_map(local, mesh=fine, in_specs=placed, out_specs=(P(ROW), P(COL)), check_vma=False)
```

time: 128 us -> 110 us (0.86)
  waiting for transfers between devices: 22.8 us -> 8.72 us
  Pallas kernels: 14.5 us -> 9.98 us
  starting transfers between devices: 22.4 us -> 25.8 us
  local copies, waits for them, and re-layouts: 3.36 us -> 1.41 us
    all_to_all x1, waiting for transfers between devices: 18.6 us -> 8.71 us  [local(): columns = lax.all_to_all(columns, ROW, 0, 0)]
    all_to_all x1 -> x0, starting transfers between devices: 9.26 us -> none  [local(): rows = lax.all_to_all(rows, QUAD, 0, 0)]
    ppermute x0 -> x3, starting transfers between devices: none -> 9.21 us  [local(): lax.ppermute(rows, QUAD, [(i, i ^ apart) for i in range(4)])]
    pallas_call x7 -> x8, Pallas kernels: 14.5 us -> 9.98 us  [the longest x1 2.5 us: local(): call(prepare_kernel, [shape((64, 16, T)), shape((OWN + 8, T))], [FAR] * 4...]
    all_to_all x1, blocking collectives: 24.5 us -> 20.2 us  [local(): parts = lax.all_to_all(parts, ROW, 0, 0)]
    all_to_all x1 -> x0, waiting for transfers between devices: 4.16 us -> none  [local(): rows = lax.all_to_all(rows, QUAD, 0, 0)]
    all_to_all x1, blocking collectives: 17.1 us -> 21 us  [local(): parts = lax.all_to_all(parts, ACROSS, 0, 0)]
    all_to_all x1, starting transfers between devices: 13.1 us -> 16.6 us  [local(): columns = lax.all_to_all(columns, ROW, 0, 0)]
  transfers between devices with their start and end apart: 2 -> 4, of which waited for: 2 -> 1; matrix products, arithmetic and copies ran while one was open for 0% -> 0% of each run, Pallas kernels for 1% -> 1%
where the time goes in v2:
time: 110 us
  blocking collectives  63.2 us (57%)
  starting transfers between devices  25.8 us (23%)
  Pallas kernels  9.98 us (9%)
  waiting for transfers between devices  8.72 us (8%)
  local copies, waits for them, and re-layouts  1.41 us (1%)
    all_to_all x2, blocking collectives, local(): parts = lax.all_to_all(parts, ALONG, 0, 0)  22.1 us
    all_to_all x1, blocking collectives, local(): parts = lax.all_to_all(parts, ACROSS, 0, 0)  21 us
    all_to_all x1, blocking collectives, local(): parts = lax.all_to_all(parts, ROW, 0, 0)  20.2 us
    all_to_all x1, starting transfers between devices, local(): columns = lax.all_to_all(columns, ROW, 0, 0)  16.6 us
    ppermute x3, starting transfers between devices, local(): lax.ppermute(rows, QUAD, [(i, i ^ apart) for i in range(4)])  9.21 us
    all_to_all x1, waiting for transfers between devices, local(): columns = lax.all_to_all(columns, ROW, 0, 0)  8.71 us
    pallas_call x1, Pallas kernels, local(): call(prepare_kernel, [shape((64, 16, T)), shape((OWN + 8, T))], [FAR] * 4...  2.5 us
    pallas_call x1, Pallas kernels, local(): call(other_costs_kernel, [shape((SIDE, SIDE)), shape((32, NB, T))], [SPEC...  2.38 us
  transfers between devices with their start and end apart: 4, of which 1 were waited for; matrix products, arithmetic and copies ran while one was open for 0% of the time, Pallas kernels for 1%

profile of v2, /device:TPU:8, one launch (start us, length us, event | category | flops | bytes accessed | tf_op | source)
XLA Modules:
  0.0 109.9 jit_solution(9433934536475209953)
XLA Ops:
  0.6 2.5 %shard_map.77 = (f32[64,16,128]{2,1,0:T(8,128)}, f32[264,128]{1,0:T(8,128)S(1)}) custom-call(s32[256]{0:T(256)} %index_hbm.1, s32[2048]{0:T(1024)} %labels_hbm.1, f32[2048,128]{1,0:T(8,128)} %pool_hbm.1, f32[2,4096]{1,0:T(2,128)} %bitcast.8), custom_call_target="tpu_custom_call" | custom-call | tf_op jit(solution)/shard_map/pallas_call | solution.py:245
  3.1 16.6 %all-to-all-start = ((f32[64,16,128]{2,1,0:T(8,128)}), f32[64,16,128]{2,1,0:T(8,128)S(1)}, u32[]{:S(2)}, u32[]{:S(2)}) async-start(f32[64,16,128]{2,1,0:T(8,128)} %get-tuple-element.19), calls=%async_computation | async-start | bytes 1048576 | tf_op jit(solution)/shard_map/all_to_all | solution.py:258
  19.7 3.4 %collective-permute-start.2 = (f32[264,128]{1,0:T(8,128)S(1)}, f32[264,128]{1,0:T(8,128)S(1)}, u32[]{:S(2)}, u32[]{:S(2)}) collective-permute-start(f32[264,128]{1,0:T(8,128)S(1)} %get-tuple-element.18.rows_ref), channel_id=1, source_target_pairs={{0,72},{8,64},{64,8},{72,0},{1,73},{9,65},{65,9},{73,1},{2,74},{10... | collective-permute-start | bytes 405512 | tf_op jit(solution)/shard_map/ppermute | solution.py:259
  23.1 2.4 %collective-permute-start.1 = (f32[264,128]{1,0:T(8,128)S(1)}, f32[264,128]{1,0:T(8,128)S(1)}, u32[]{:S(2)}, u32[]{:S(2)}) collective-permute-start(f32[264,128]{1,0:T(8,128)S(1)} %get-tuple-element.18.rows_ref), channel_id=1, source_target_pairs={{0,64},{8,72},{64,0},{72,8},{1,65},{9,73},{65,1},{73,9},{2,66},{10... | collective-permute-start | bytes 405512 | tf_op jit(solution)/shard_map/ppermute | solution.py:259
  25.5 3.5 %collective-permute-start = (f32[264,128]{1,0:T(8,128)S(1)}, f32[264,128]{1,0:T(8,128)S(1)}, u32[]{:S(2)}, u32[]{:S(2)}) collective-permute-start(f32[264,128]{1,0:T(8,128)S(1)} %get-tuple-element.18.rows_ref), channel_id=1, source_target_pairs={{0,8},{8,0},{64,72},{72,64},{1,9},{9,1},{65,73},{73,65},{2,10},{10... | collective-permute-start | bytes 405512 | tf_op jit(solution)/shard_map/ppermute | solution.py:259
  29.0 0.0 copy-start
  29.0 0.7 copy-done
  29.7 0.0 copy-start.1
  29.7 0.7 copy-done.1
  30.4 0.2 shard_map.78.kinds_ref
  30.6 8.7 %all-to-all-done = f32[64,16,128]{2,1,0:T(8,128)S(1)} async-done(((f32[64,16,128]{2,1,0:T(8,128)}), f32[64,16,128]{2,1,0:T(8,128)S(1)}, u32[]{:S(2)}, u32[]{:S(2)}) %all-to-all-start) | async-done | bytes 524320 | tf_op jit(solution)/shard_map/all_to_all | solution.py:258
  39.3 1.2 %shard_map.79 = (f32[256,1024]{1,0:T(8,128)S(1)}, f32[8,128]{1,0:T(8,128)S(1)}, bf16[896,1024]{1,0:T(8,128)(2,1)S(1)}, f32[8,1024]{1,0:T(8,128)S(1)}) custom-call(f32[264,128]{1,0:T(8,128)S(1)} %get-tuple-element.18.rows_ref, f32[1024,128]{1,0:T(8,128)S(1)} %bitcast.6, bf16[128,1024]{1,0:T(8,128)(2,1)S(1)} %shard_map.78.kinds_ref), custom_call_target="tpu_custom_call" | custom-call | tf_op jit(solution)/shard_map/pallas_call | solution.py:265
  40.5 0.0 collective-permute-done.2.rows3_ref
  40.5 0.0 collective-permute-done.1.rows2_ref
  40.5 0.0 collective-permute-done.rows1_ref
  40.6 2.4 %shard_map.80 = (f32[1024,1024]{1,0:T(8,128)S(1)}, f32[32,8,128]{2,1,0:T(8,128)S(1)}) custom-call(f32[264,128]{1,0:T(8,128)S(1)} %collective-permute-done.rows1_ref, f32[264,128]{1,0:T(8,128)S(1)} %collective-permute-done.1.rows2_ref, f32[264,128]{1,0:T(8,128)S(1)} %collective-permute-done.2.rows3_ref, bf16[896,1024]{1,0:T(8,128)(2,1)S(1)} %get-tuple-element.22.b_ref, ...), custom_call_target="tpu_custom_call" | custom-call | tf_op jit(solution)/shard_map/pallas_call | solution.py:271
  42.9 11.9 %all_to_all.25.parts_ref = f32[32,8,128]{2,1,0:T(8,128)S(1)} all-to-all(f32[32,8,128]{2,1,0:T(8,128)S(1)} %get-tuple-element.26), channel_id=1, replica_groups=mesh['z2'=2,'z1'=2,'z0'=2,'y2'=2,'y1'=2,'y0'=2,'x'=4,'core'=2] {'z0','y0..., dimensions={0} | all-to-all | bytes 262144 | tf_op jit(solution)/shard_map/all_to_all | solution.py:277
  54.9 1.0 shard_map.81
  55.9 21.0 %all_to_all.26.parts_ref = f32[16,8,128]{2,1,0:T(8,128)S(1)} all-to-all(f32[16,8,128]{2,1,0:T(8,128)S(1)} %shard_map.81), channel_id=1, replica_groups=mesh['z2'=2,'z1'=2,'z0'=2,'y2'=2,'y1'=2,'y0'=2,'x'=4,'core'=2] {'z2','z1..., dimensions={0} | all-to-all | bytes 131072 | tf_op jit(solution)/shard_map/all_to_all | solution.py:279
  76.9 0.9 shard_map.82
  77.8 10.2 %all_to_all.27.parts_ref = f32[32,8,128]{2,1,0:T(8,128)S(1)} all-to-all(f32[32,8,128]{2,1,0:T(8,128)S(1)} %shard_map.82), channel_id=1, replica_groups=mesh['z2'=2,'z1'=2,'z0'=2,'y2'=2,'y1'=2,'y0'=2,'x'=4,'core'=2] {'z0','y0..., dimensions={0} | all-to-all | bytes 262144 | tf_op jit(solution)/shard_map/all_to_all | solution.py:281
  87.9 1.1 shard_map.83
  89.0 20.2 %all_to_all.28.parts_ref = f32[64,1,1152]{2,1,0:T(1,128)S(1)} all-to-all(f32[64,1,1152]{2,1,0:T(1,128)S(1)} %get-tuple-element.28), channel_id=1, replica_groups=mesh['z2'=2,'z1'=2,'z0'=2,'y2'=2,'y1'=2,'y0'=2,'x'=4,'core'=2] {'z2','z1..., dimensions={0} | all-to-all | bytes 589824 | tf_op jit(solution)/shard_map/all_to_all | solution.py:285
  109.2 0.7 shard_map.84
Async XLA Ops:
  3.1 36.2 %all-to-all-start = ((f32[64,16,128]{2,1,0:T(8,128)}), f32[64,16,128]{2,1,0:T(8,128)S(1)}, u32[]{:S(2)}, u32[]{:S(2)}) async-start(f32[64,16,128]{2,1,0:T(8,128)} %get-tuple-element.19), calls=%async_computation | async-start | bytes 1048576 | tf_op jit(solution)/shard_map/all_to_all | solution.py:258
  19.7 20.8 %collective-permute-start.2 = (f32[264,128]{1,0:T(8,128)S(1)}, f32[264,128]{1,0:T(8,128)S(1)}, u32[]{:S(2)}, u32[]{:S(2)}) collective-permute-start(f32[264,128]{1,0:T(8,128)S(1)} %get-tuple-element.18.rows_ref), channel_id=1, source_target_pairs={{0,72},{8,64},{64,8},{72,0},{1,73},{9,65},{65,9},{73,1},{2,74},{10... | collective-permute-start | bytes 405512 | tf_op jit(solution)/shard_map/ppermute | solution.py:259
  23.1 17.4 %collective-permute-start.1 = (f32[264,128]{1,0:T(8,128)S(1)}, f32[264,128]{1,0:T(8,128)S(1)}, u32[]{:S(2)}, u32[]{:S(2)}) collective-permute-start(f32[264,128]{1,0:T(8,128)S(1)} %get-tuple-element.18.rows_ref), channel_id=1, source_target_pairs={{0,64},{8,72},{64,0},{72,8},{1,65},{9,73},{65,1},{73,9},{2,66},{10... | collective-permute-start | bytes 405512 | tf_op jit(solution)/shard_map/ppermute | solution.py:259
  25.5 15.1 %collective-permute-start = (f32[264,128]{1,0:T(8,128)S(1)}, f32[264,128]{1,0:T(8,128)S(1)}, u32[]{:S(2)}, u32[]{:S(2)}) collective-permute-start(f32[264,128]{1,0:T(8,128)S(1)} %get-tuple-element.18.rows_ref), channel_id=1, source_target_pairs={{0,8},{8,0},{64,72},{72,64},{1,9},{9,1},{65,73},{73,65},{2,10},{10... | collective-permute-start | bytes 405512 | tf_op jit(solution)/shard_map/ppermute | solution.py:259
  29.0 0.7 copy-start
  29.7 0.7 copy-start.1

commit v3 on v2

--- a/solution.py
+++ b/solution.py
@@ -18,6 +18,19 @@
 ACROSS = ("z2", "z1", "y2", "y1")
 ALONG = QUAD + COL
 
+FIRST = (6, 4)
+LATER = (4, 4)
+
+
+def turned(z_size, y_size, z_first, y_first):
+    return [[(z + z_first) % z_size * y_size + (y + y_first) % y_size for z in range(z_size) for y in range(y_size)]]
+
+
+FIRST_ROW_ORDER = turned(8, 8, *FIRST)
+ROW_ORDER = turned(8, 8, *LATER)
+ACROSS_ORDER = turned(4, 4, LATER[0] // 2, LATER[1] // 2)
+ALONG_ORDER = [[(quarter ^ 3) * 8 + (x + 2) % 4 * 2 + core for quarter in range(4) for x in range(4) for core in range(2)]]
+
 T = 128
 NB = 8
 SIDE = NB * T
@@ -39,6 +52,11 @@
     return ((z * 2 + quarter // 2) * 4 + y) * 2 + quarter % 2
 
 
+def in_order(y):
+    places = [(z - FIRST[0]) % 8 * 2 + (half - FIRST[1] // 4) % 2 for z in range(8) for half in range(2)]
+    return jnp.concatenate([y[8 * place : 8 * place + 8] for place in places], axis=0)
+
+
 def tree(op, xs):
     xs = list(xs)
     while len(xs) > 1:
@@ -62,14 +80,10 @@
         out_ref[k] = part
 
 
-def prepare_kernel(
-    index_hbm, labels_hbm, pool_hbm, val_hbm, columns_ref, rows_ref, index_ref, labels_ref, pool_ref, val_ref, column_ref, sems
-):
-    moves = [(val_hbm, val_ref), (index_hbm, index_ref), (labels_hbm, labels_ref), (pool_hbm, pool_ref)]
-    copies = [pltpu.make_async_copy(a, b, sems.at[k]) for k, (a, b) in enumerate(moves)]
-    for copy in copies:
-        copy.start()
-    copies[0].wait()
+def columns_kernel(val_hbm, columns_ref, val_ref, sem):
+    copy = pltpu.make_async_copy(val_hbm, val_ref, sem)
+    copy.start()
+    copy.wait()
     for quarter in range(4):
         first = member(quarter, 0, 0)
         for block in range(NB):
@@ -81,7 +95,14 @@
             for y in range(4):
                 if z or y:
                     columns_ref[member(quarter, z, y)] = whole
-    for copy in copies[1:]:
+
+
+def rows_kernel(index_hbm, labels_hbm, pool_hbm, rows_ref, index_ref, labels_ref, pool_ref, column_ref, sems):
+    moves = [(index_hbm, index_ref), (labels_hbm, labels_ref), (pool_hbm, pool_ref)]
+    copies = [pltpu.make_async_copy(a, b, sems.at[k]) for k, (a, b) in enumerate(moves)]
+    for copy in copies:
+        copy.start()
+    for copy in copies:
         copy.wait()
 
     def step(i, carry):
@@ -141,7 +162,7 @@
 def own_costs_kernel(rows_ref, val_ref, kinds_ref, cost_ref, part_ref, b_ref, squares_ref, piece_ref):
     for block in range(NB):
         lanes = slice(block * T, (block + 1) * T)
-        y = val_ref[pl.ds(block, T, stride=NB), :]
+        y = in_order(val_ref[pl.ds(block, T, stride=NB), :])
         hi, mid, low = split3(y)
         for k, part in enumerate((hi, mid, hi, low, hi, mid)):
             b_ref[k * T : (k + 1) * T, lanes] = part
@@ -225,6 +246,10 @@
     return pltpu.VMEM(shape, dtype)
 
 
+def far(x):
+    return pltpu.with_memory_space_constraint(x, pltpu.HBM)
+
+
 def shape(dims, dtype=F32):
     return jax.ShapeDtypeStruct(dims, dtype)
 
@@ -242,20 +267,23 @@
 
 def local(pool, window_index, pool_labels, val_embed, val_labels, class_cost):
     quarter = lax.axis_index(QUAD).astype(jnp.int32).reshape(1)
-    columns, rows = call(
-        prepare_kernel,
-        [shape((64, 16, T)), shape((OWN + 8, T))],
-        [FAR] * 4,
+    (columns,) = call(
+        columns_kernel, [shape((64, 16, T))], [FAR], [vmem((2, 4096)), pltpu.SemaphoreType.DMA(())]
+    )(far(val_embed.T))
+    columns, window_index = lax.optimization_barrier((columns, window_index))
+    (rows,) = call(
+        rows_kernel,
+        [shape((OWN + 8, T))],
+        [FAR] * 3,
         [
             pltpu.SMEM(window_index.shape, jnp.int32),
             pltpu.SMEM(pool_labels.shape, jnp.int32),
             vmem(pool.shape),
-            vmem((2, 4096)),
             vmem((OWN, T)),
-            pltpu.SemaphoreType.DMA((4,)),
+            pltpu.SemaphoreType.DMA((3,)),
         ],
-    )(*[pltpu.with_memory_space_constraint(x, pltpu.HBM) for x in (window_index, pool_labels, pool, val_embed.T)])
-    columns = lax.all_to_all(columns, ROW, 0, 0)
+    )(far(window_index), far(pool_labels), far(pool))
+    columns = lax.all_to_all(columns, ROW, 0, 0, axis_index_groups=FIRST_ROW_ORDER)
     others = [lax.ppermute(rows, QUAD, [(i, i ^ apart) for i in range(4)]) for apart in (1, 2, 3)]
     rows, val_labels, class_cost = lax.optimization_barrier((rows, val_labels, class_cost))
     (kinds,) = call(labels_kernel, [shape((T, SIDE), BF16)], [SCALARS, SPEC, SPEC])(
@@ -274,15 +302,15 @@
         [SPEC] * 5 + [SCALARS] + [SPEC] * 2,
         [part, vmem((3, 2, T, T))],
     )(*others, b, squares, quarter, own, part_own)
-    parts = lax.all_to_all(parts, ALONG, 0, 0)
+    parts = lax.all_to_all(parts, ALONG, 0, 0, axis_index_groups=ALONG_ORDER)
     (parts,) = call(columns_step_kernel, [shape((16, NB, T))], [SPEC] * 2, [wide, part])(parts, cost)
-    parts = lax.all_to_all(parts, ACROSS, 0, 0)
+    parts = lax.all_to_all(parts, ACROSS, 0, 0, axis_index_groups=ACROSS_ORDER)
     (parts,) = call(rows_step_kernel, [shape((32, NB, T))], [SPEC] * 2, [piece, part])(parts, cost)
-    parts = lax.all_to_all(parts, ALONG, 0, 0)
+    parts = lax.all_to_all(parts, ALONG, 0, 0, axis_index_groups=ALONG_ORDER)
     parts, f = call(
         last_columns_kernel, [shape((64, 1, SIDE + T)), shape((NB, T))], [SPEC] * 2, [wide, part, vmem((1, SIDE + T))]
     )(parts, cost)
-    parts = lax.all_to_all(parts, ROW, 0, 0)
+    parts = lax.all_to_all(parts, ROW, 0, 0, axis_index_groups=ROW_ORDER)
     value, potential = call(finish_kernel, [shape((2, T)), shape((4, 1, SIDE))], [SPEC, SPEC, SCALARS])(parts, f, quarter)
     return value.reshape(256), potential.reshape(4096)
 

time: 110 us -> 103 us (0.936)
  blocking collectives: 63.2 us -> 57 us
  waiting for transfers between devices: 8.72 us -> 5.54 us
    all_to_all x4, blocking collectives: 63.2 us -> 57 us  [the longest x1 21.2 us: local(): parts = lax.all_to_all(parts, ROW, 0, 0, axis_index_groups=ROW_ORDER)]
    all_to_all x1, waiting for transfers between devices: 8.71 us -> 3.58 us  [local(): lax.all_to_all(columns, ROW, 0, 0, axis_index_groups=FIRST_ROW_ORDER)]
    ppermute x3, waiting for transfers between devices: 0.01 us -> 1.96 us  [local(): lax.ppermute(rows, QUAD, [(i, i ^ apart) for i in range(4)])]
    pallas_call x1 -> x2, Pallas kernels: 2.5 us -> 3.36 us  [the longest x1 1.75 us: local(): call(rows_kernel, [shape((OWN + 8, T))], [FAR] * 3, [pltpu.SMEM(window_in...]
  transfers between devices with their start and end apart: 4 -> 4, of which waited for: 1 -> 3; matrix products, arithmetic and copies ran while one was open for 0% -> 0% of each run, Pallas kernels for 1% -> 3%
where the time goes in v3:
time: 103 us; the launch traced here: 102 us
  blocking collectives  57 us (55%)
  starting transfers between devices  26.7 us (26%)
  Pallas kernels  10.9 us (11%)
  waiting for transfers between devices  5.54 us (5%)
  local copies, waits for them, and re-layouts  1.41 us (1%)
    all_to_all x1, blocking collectives, local(): parts = lax.all_to_all(parts, ROW, 0, 0, axis_index_groups=ROW_ORDER)  21.2 us
    all_to_all x2, blocking collectives, local(): parts = lax.all_to_all(parts, ALONG, 0, 0, axis_index_groups=ALONG_ORDER)  21 us
    all_to_all x1, starting transfers between devices, local(): lax.all_to_all(columns, ROW, 0, 0, axis_index_groups=FIRST_ROW_ORDER)  17.5 us
    all_to_all x1, blocking collectives, local(): parts = lax.all_to_all(parts, ACROSS, 0, 0, axis_index_groups=ACROSS_ORDER)  14.7 us
    ppermute x3, starting transfers between devices, local(): lax.ppermute(rows, QUAD, [(i, i ^ apart) for i in range(4)])  9.21 us
    all_to_all x1, waiting for transfers between devices, local(): lax.all_to_all(columns, ROW, 0, 0, axis_index_groups=FIRST_ROW_ORDER)  3.58 us
    pallas_call x1, Pallas kernels, local(): call(other_costs_kernel, [shape((SIDE, SIDE)), shape((32, NB, T))], [SPEC...  2.38 us
  transfers between devices with their start and end apart: 4, of which 3 were waited for; matrix products, arithmetic and copies ran while one was open for 0% of the time, Pallas kernels for 3%

profile of v3, /device:TPU:8, one launch (start us, length us, event | category | flops | bytes accessed | tf_op | source)
XLA Modules:
  0.0 102.2 jit_solution(1795049160086725667)
XLA Ops:
  0.6 1.6 %shard_map.77 = f32[64,16,128]{2,1,0:T(8,128)} custom-call(f32[2,4096]{1,0:T(2,128)} %bitcast.8), custom_call_target="tpu_custom_call" | custom-call | tf_op jit(solution)/shard_map/pallas_call | solution.py:270
  2.2 17.5 %all-to-all-start = ((f32[64,16,128]{2,1,0:T(8,128)}), f32[64,16,128]{2,1,0:T(8,128)S(1)}, u32[]{:S(2)}, u32[]{:S(2)}) async-start(f32[64,16,128]{2,1,0:T(8,128)} %shard_map.77), calls=%async_computation | async-start | bytes 1048576 | tf_op jit(solution)/shard_map/all_to_all | solution.py:286
  19.7 1.7 %shard_map.78.rows_ref = f32[264,128]{1,0:T(8,128)S(1)} custom-call(s32[256]{0:T(256)} %index_hbm, s32[2048]{0:T(1024)} %labels_hbm.1, f32[2048,128]{1,0:T(8,128)} %pool_hbm.1), custom_call_target="tpu_custom_call" | custom-call | tf_op jit(solution)/shard_map/pallas_call | solution.py:274
  21.5 4.3 %collective-permute-start.2 = (f32[264,128]{1,0:T(8,128)S(1)}, f32[264,128]{1,0:T(8,128)S(1)}, u32[]{:S(2)}, u32[]{:S(2)}) collective-permute-start(f32[264,128]{1,0:T(8,128)S(1)} %shard_map.78.rows_ref), channel_id=1, source_target_pairs={{0,72},{8,64},{64,8},{72,0},{1,73},{9,65},{65,9},{73,1},{2,74},{10... | collective-permute-start | bytes 405512 | tf_op jit(solution)/shard_map/ppermute | solution.py:287
  25.8 2.4 %collective-permute-start.1 = (f32[264,128]{1,0:T(8,128)S(1)}, f32[264,128]{1,0:T(8,128)S(1)}, u32[]{:S(2)}, u32[]{:S(2)}) collective-permute-start(f32[264,128]{1,0:T(8,128)S(1)} %shard_map.78.rows_ref), channel_id=1, source_target_pairs={{0,64},{8,72},{64,0},{72,8},{1,65},{9,73},{65,1},{73,9},{2,66},{10... | collective-permute-start | bytes 405512 | tf_op jit(solution)/shard_map/ppermute | solution.py:287
  28.3 2.5 %collective-permute-start = (f32[264,128]{1,0:T(8,128)S(1)}, f32[264,128]{1,0:T(8,128)S(1)}, u32[]{:S(2)}, u32[]{:S(2)}) collective-permute-start(f32[264,128]{1,0:T(8,128)S(1)} %shard_map.78.rows_ref), channel_id=1, source_target_pairs={{0,8},{8,0},{64,72},{72,64},{1,9},{9,1},{65,73},{73,65},{2,10},{10... | collective-permute-start | bytes 405512 | tf_op jit(solution)/shard_map/ppermute | solution.py:287
  30.7 0.0 copy-start
  30.8 0.7 copy-done
  31.5 0.0 copy-start.1
  31.5 0.7 copy-done.1
  32.2 0.2 shard_map.79.kinds_ref
  32.4 3.6 %all-to-all-done = f32[64,16,128]{2,1,0:T(8,128)S(1)} async-done(((f32[64,16,128]{2,1,0:T(8,128)}), f32[64,16,128]{2,1,0:T(8,128)S(1)}, u32[]{:S(2)}, u32[]{:S(2)}) %all-to-all-start) | async-done | bytes 524320 | tf_op jit(solution)/shard_map/all_to_all | solution.py:286
  36.0 1.2 %shard_map.80 = (f32[256,1024]{1,0:T(8,128)S(1)}, f32[8,128]{1,0:T(8,128)S(1)}, bf16[896,1024]{1,0:T(8,128)(2,1)S(1)}, f32[8,1024]{1,0:T(8,128)S(1)}) custom-call(f32[264,128]{1,0:T(8,128)S(1)} %shard_map.78.rows_ref, f32[1024,128]{1,0:T(8,128)S(1)} %bitcast.6, bf16[128,1024]{1,0:T(8,128)(2,1)S(1)} %shard_map.79.kinds_ref), custom_call_target="tpu_custom_call" | custom-call | tf_op jit(solution)/shard_map/pallas_call | solution.py:293
  37.2 0.2 collective-permute-done.2.rows3_ref
  37.4 1.8 %collective-permute-done.1.rows2_ref = f32[264,128]{1,0:T(8,128)S(1)} collective-permute-done((f32[264,128]{1,0:T(8,128)S(1)}, f32[264,128]{1,0:T(8,128)S(1)}, u32[]{:S(2)}, u32[]{:S(2)}) %collective-permute-start.1) | collective-permute-done | bytes 135200 | tf_op jit(solution)/shard_map/ppermute | solution.py:287
  39.1 0.0 collective-permute-done.rows1_ref
  39.1 2.4 %shard_map.81 = (f32[1024,1024]{1,0:T(8,128)S(1)}, f32[32,8,128]{2,1,0:T(8,128)S(1)}) custom-call(f32[264,128]{1,0:T(8,128)S(1)} %collective-permute-done.rows1_ref, f32[264,128]{1,0:T(8,128)S(1)} %collective-permute-done.1.rows2_ref, f32[264,128]{1,0:T(8,128)S(1)} %collective-permute-done.2.rows3_ref, bf16[896,1024]{1,0:T(8,128)(2,1)S(1)} %get-tuple-element.22.b_ref, ...), custom_call_target="tpu_custom_call" | custom-call | tf_op jit(solution)/shard_map/pallas_call | solution.py:299
  41.5 10.9 %all_to_all.25.parts_ref = f32[32,8,128]{2,1,0:T(8,128)S(1)} all-to-all(f32[32,8,128]{2,1,0:T(8,128)S(1)} %get-tuple-element.26), channel_id=1, replica_groups={{76,77,78,79,72,73,74,75,68,69,70,71,64,65,66,67,12,13,14,15,8,9,10,11,..., dimensions={0} | all-to-all | bytes 262144 | tf_op jit(solution)/shard_map/all_to_all | solution.py:305
  52.4 1.0 %shard_map.82 = f32[16,8,128]{2,1,0:T(8,128)S(1)} custom-call(f32[32,8,128]{2,1,0:T(8,128)S(1)} %all_to_all.25.parts_ref, f32[1024,1024]{1,0:T(8,128)S(1)} %get-tuple-element.27.cost_ref), custom_call_target="tpu_custom_call" | custom-call | tf_op jit(solution)/shard_map/pallas_call | solution.py:306
  53.5 14.7 %all_to_all.26.parts_ref = f32[16,8,128]{2,1,0:T(8,128)S(1)} all-to-all(f32[16,8,128]{2,1,0:T(8,128)S(1)} %shard_map.82), channel_id=1, replica_groups={{288,304,256,272,416,432,384,400,32,48,0,16,160,176,128,144},{289,305,2..., dimensions={0} | all-to-all | bytes 131072 | tf_op jit(solution)/shard_map/all_to_all | solution.py:307
  68.2 0.9 shard_map.83
  69.1 10.1 %all_to_all.27.parts_ref = f32[32,8,128]{2,1,0:T(8,128)S(1)} all-to-all(f32[32,8,128]{2,1,0:T(8,128)S(1)} %shard_map.83), channel_id=1, replica_groups={{76,77,78,79,72,73,74,75,68,69,70,71,64,65,66,67,12,13,14,15,8,9,10,11,..., dimensions={0} | all-to-all | bytes 262144 | tf_op jit(solution)/shard_map/all_to_all | solution.py:309
  79.2 1.1 %shard_map.84 = (f32[64,1,1152]{2,1,0:T(1,128)S(1)}, f32[8,128]{1,0:T(8,128)S(1)}) custom-call(f32[32,8,128]{2,1,0:T(8,128)S(1)} %all_to_all.27.parts_ref, f32[1024,1024]{1,0:T(8,128)S(1)} %get-tuple-element.27.cost_ref), custom_call_target="tpu_custom_call" | custom-call | tf_op jit(solution)/shard_map/pallas_call | solution.py:310
  80.3 21.2 %all_to_all.28.parts_ref = f32[64,1,1152]{2,1,0:T(1,128)S(1)} all-to-all(f32[64,1,1152]{2,1,0:T(1,128)S(1)} %get-tuple-element.28), channel_id=1, replica_groups={{288,296,304,312,256,264,272,280,352,360,368,376,320,328,336,344,416,42..., dimensions={0} | all-to-all | bytes 589824 | tf_op jit(solution)/shard_map/all_to_all | solution.py:313
  101.5 0.7 shard_map.85
Async XLA Ops:
  2.2 33.7 %all-to-all-start = ((f32[64,16,128]{2,1,0:T(8,128)}), f32[64,16,128]{2,1,0:T(8,128)S(1)}, u32[]{:S(2)}, u32[]{:S(2)}) async-start(f32[64,16,128]{2,1,0:T(8,128)} %shard_map.77), calls=%async_computation | async-start | bytes 1048576 | tf_op jit(solution)/shard_map/all_to_all | solution.py:286
  21.5 15.9 %collective-permute-start.2 = (f32[264,128]{1,0:T(8,128)S(1)}, f32[264,128]{1,0:T(8,128)S(1)}, u32[]{:S(2)}, u32[]{:S(2)}) collective-permute-start(f32[264,128]{1,0:T(8,128)S(1)} %shard_map.78.rows_ref), channel_id=1, source_target_pairs={{0,72},{8,64},{64,8},{72,0},{1,73},{9,65},{65,9},{73,1},{2,74},{10... | collective-permute-start | bytes 405512 | tf_op jit(solution)/shard_map/ppermute | solution.py:287
  25.8 13.3 %collective-permute-start.1 = (f32[264,128]{1,0:T(8,128)S(1)}, f32[264,128]{1,0:T(8,128)S(1)}, u32[]{:S(2)}, u32[]{:S(2)}) collective-permute-start(f32[264,128]{1,0:T(8,128)S(1)} %shard_map.78.rows_ref), channel_id=1, source_target_pairs={{0,64},{8,72},{64,0},{72,8},{1,65},{9,73},{65,1},{73,9},{2,66},{10... | collective-permute-start | bytes 405512 | tf_op jit(solution)/shard_map/ppermute | solution.py:287
  28.3 10.9 %collective-permute-start = (f32[264,128]{1,0:T(8,128)S(1)}, f32[264,128]{1,0:T(8,128)S(1)}, u32[]{:S(2)}, u32[]{:S(2)}) collective-permute-start(f32[264,128]{1,0:T(8,128)S(1)} %shard_map.78.rows_ref), channel_id=1, source_target_pairs={{0,8},{8,0},{64,72},{72,64},{1,9},{9,1},{65,73},{73,65},{2,10},{10... | collective-permute-start | bytes 405512 | tf_op jit(solution)/shard_map/ppermute | solution.py:287
  30.7 0.7 copy-start
  31.5 0.7 copy-start.1

commit v4 on v3

--- a/solution.py
+++ b/solution.py
@@ -18,18 +18,16 @@
 ACROSS = ("z2", "z1", "y2", "y1")
 ALONG = QUAD + COL
 
-FIRST = (6, 4)
-LATER = (4, 4)
+FIRST = (4, 4)
 
 
 def turned(z_size, y_size, z_first, y_first):
     return [[(z + z_first) % z_size * y_size + (y + y_first) % y_size for z in range(z_size) for y in range(y_size)]]
 
 
-FIRST_ROW_ORDER = turned(8, 8, *FIRST)
-ROW_ORDER = turned(8, 8, *LATER)
-ACROSS_ORDER = turned(4, 4, LATER[0] // 2, LATER[1] // 2)
-ALONG_ORDER = [[(quarter ^ 3) * 8 + (x + 2) % 4 * 2 + core for quarter in range(4) for x in range(4) for core in range(2)]]
+ROW_ORDER = turned(8, 8, *FIRST)
+ACROSS_ORDER = turned(4, 4, FIRST[0] // 2, FIRST[1] // 2)
+ALONG_ORDER = [[(quarter ^ 3) * 8 + (x + 2) % 4 * 2 + (1 - core) for quarter in range(4) for x in range(4) for core in range(2)]]
 
 T = 128
 NB = 8
@@ -283,7 +281,7 @@
             pltpu.SemaphoreType.DMA((3,)),
         ],
     )(far(window_index), far(pool_labels), far(pool))
-    columns = lax.all_to_all(columns, ROW, 0, 0, axis_index_groups=FIRST_ROW_ORDER)
+    columns = lax.all_to_all(columns, ROW, 0, 0, axis_index_groups=ROW_ORDER)
     others = [lax.ppermute(rows, QUAD, [(i, i ^ apart) for i in range(4)]) for apart in (1, 2, 3)]
     rows, val_labels, class_cost = lax.optimization_barrier((rows, val_labels, class_cost))
     (kinds,) = call(labels_kernel, [shape((T, SIDE), BF16)], [SCALARS, SPEC, SPEC])(

time: 103 us -> 102 us (level)
  blocking collectives: 57 us -> 55.5 us
  starting transfers between devices: 26.7 us -> 28.1 us
    all_to_all x1, waiting for transfers between devices: 3.58 us -> 1.46 us  [local(): columns = lax.all_to_all(columns, ROW, 0, 0, axis_index_groups=ROW_ORDER)]
    all_to_all x2, blocking collectives: 21 us -> 19.6 us  [local(): parts = lax.all_to_all(parts, ALONG, 0, 0, axis_index_groups=ALONG_ORDER)]
    all_to_all x1, starting transfers between devices: 17.5 us -> 18.9 us  [local(): columns = lax.all_to_all(columns, ROW, 0, 0, axis_index_groups=ROW_ORDER)]
    ppermute x3, waiting for transfers between devices: 1.96 us -> 3.14 us  [local(): lax.ppermute(rows, QUAD, [(i, i ^ apart) for i in range(4)])]
  transfers between devices with their start and end apart: 4 -> 4, of which waited for: 3 -> 4; matrix products, arithmetic and copies ran while one was open for 0% -> 0% of each run, Pallas kernels for 3% -> 3%
where the time goes in v4:
time: 102 us; the launch traced here: 101 us
  blocking collectives  55.5 us (54%)
  starting transfers between devices  28.1 us (28%)
  Pallas kernels  10.9 us (11%)
  waiting for transfers between devices  4.6 us (5%)
  local copies, waits for them, and re-layouts  1.41 us (1%)
    all_to_all x1, blocking collectives, local(): parts = lax.all_to_all(parts, ROW, 0, 0, axis_index_groups=ROW_ORDER)  21.1 us
    all_to_all x2, blocking collectives, local(): parts = lax.all_to_all(parts, ALONG, 0, 0, axis_index_groups=ALONG_ORDER)  19.6 us
    all_to_all x1, starting transfers between devices, local(): columns = lax.all_to_all(columns, ROW, 0, 0, axis_index_groups=ROW_ORDER)  18.9 us
    all_to_all x1, blocking collectives, local(): parts = lax.all_to_all(parts, ACROSS, 0, 0, axis_index_groups=ACROSS_ORDER)  14.7 us
    ppermute x3, starting transfers between devices, local(): lax.ppermute(rows, QUAD, [(i, i ^ apart) for i in range(4)])  9.21 us
    ppermute x3, waiting for transfers between devices, local(): lax.ppermute(rows, QUAD, [(i, i ^ apart) for i in range(4)])  3.14 us
    pallas_call x1, Pallas kernels, local(): call(other_costs_kernel, [shape((SIDE, SIDE)), shape((32, NB, T))], [SPEC...  2.38 us
  transfers between devices with their start and end apart: 4, of which 4 were waited for; matrix products, arithmetic and copies ran while one was open for 0% of the time, Pallas kernels for 3%

profile of v4, /device:TPU:8, one launch (start us, length us, event | category | flops | bytes accessed | tf_op | source)
XLA Modules:
  0.0 101.1 jit_solution(6155015677320559560)
XLA Ops:
  0.6 1.6 %shard_map.77 = f32[64,16,128]{2,1,0:T(8,128)} custom-call(f32[2,4096]{1,0:T(2,128)} %bitcast.8), custom_call_target="tpu_custom_call" | custom-call | tf_op jit(solution)/shard_map/pallas_call | solution.py:268
  2.2 18.9 %all-to-all-start = ((f32[64,16,128]{2,1,0:T(8,128)}), f32[64,16,128]{2,1,0:T(8,128)S(1)}, u32[]{:S(2)}, u32[]{:S(2)}) async-start(f32[64,16,128]{2,1,0:T(8,128)} %shard_map.77), calls=%async_computation | async-start | bytes 1048576 | tf_op jit(solution)/shard_map/all_to_all | solution.py:284
  21.1 1.7 %shard_map.78.rows_ref = f32[264,128]{1,0:T(8,128)S(1)} custom-call(s32[256]{0:T(256)} %index_hbm, s32[2048]{0:T(1024)} %labels_hbm.1, f32[2048,128]{1,0:T(8,128)} %pool_hbm.1), custom_call_target="tpu_custom_call" | custom-call | tf_op jit(solution)/shard_map/pallas_call | solution.py:272
  22.9 3.4 %collective-permute-start.2 = (f32[264,128]{1,0:T(8,128)S(1)}, f32[264,128]{1,0:T(8,128)S(1)}, u32[]{:S(2)}, u32[]{:S(2)}) collective-permute-start(f32[264,128]{1,0:T(8,128)S(1)} %shard_map.78.rows_ref), channel_id=1, source_target_pairs={{0,72},{8,64},{64,8},{72,0},{1,73},{9,65},{65,9},{73,1},{2,74},{10... | collective-permute-start | bytes 405512 | tf_op jit(solution)/shard_map/ppermute | solution.py:285
  26.3 3.3 %collective-permute-start.1 = (f32[264,128]{1,0:T(8,128)S(1)}, f32[264,128]{1,0:T(8,128)S(1)}, u32[]{:S(2)}, u32[]{:S(2)}) collective-permute-start(f32[264,128]{1,0:T(8,128)S(1)} %shard_map.78.rows_ref), channel_id=1, source_target_pairs={{0,64},{8,72},{64,0},{72,8},{1,65},{9,73},{65,1},{73,9},{2,66},{10... | collective-permute-start | bytes 405512 | tf_op jit(solution)/shard_map/ppermute | solution.py:285
  29.6 2.5 %collective-permute-start = (f32[264,128]{1,0:T(8,128)S(1)}, f32[264,128]{1,0:T(8,128)S(1)}, u32[]{:S(2)}, u32[]{:S(2)}) collective-permute-start(f32[264,128]{1,0:T(8,128)S(1)} %shard_map.78.rows_ref), channel_id=1, source_target_pairs={{0,8},{8,0},{64,72},{72,64},{1,9},{9,1},{65,73},{73,65},{2,10},{10... | collective-permute-start | bytes 405512 | tf_op jit(solution)/shard_map/ppermute | solution.py:285
  32.1 0.0 copy-start
  32.1 0.7 copy-done
  32.8 0.0 copy-start.1
  32.8 0.7 copy-done.1
  33.5 0.2 shard_map.79.kinds_ref
  33.8 1.5 %all-to-all-done = f32[64,16,128]{2,1,0:T(8,128)S(1)} async-done(((f32[64,16,128]{2,1,0:T(8,128)}), f32[64,16,128]{2,1,0:T(8,128)S(1)}, u32[]{:S(2)}, u32[]{:S(2)}) %all-to-all-start) | async-done | bytes 524320 | tf_op jit(solution)/shard_map/all_to_all | solution.py:284
  35.2 1.2 %shard_map.80 = (f32[256,1024]{1,0:T(8,128)S(1)}, f32[8,128]{1,0:T(8,128)S(1)}, bf16[896,1024]{1,0:T(8,128)(2,1)S(1)}, f32[8,1024]{1,0:T(8,128)S(1)}) custom-call(f32[264,128]{1,0:T(8,128)S(1)} %shard_map.78.rows_ref, f32[1024,128]{1,0:T(8,128)S(1)} %bitcast.6, bf16[128,1024]{1,0:T(8,128)(2,1)S(1)} %shard_map.79.kinds_ref), custom_call_target="tpu_custom_call" | custom-call | tf_op jit(solution)/shard_map/pallas_call | solution.py:291
  36.4 1.3 %collective-permute-done.2.rows3_ref = f32[264,128]{1,0:T(8,128)S(1)} collective-permute-done((f32[264,128]{1,0:T(8,128)S(1)}, f32[264,128]{1,0:T(8,128)S(1)}, u32[]{:S(2)}, u32[]{:S(2)}) %collective-permute-start.2) | collective-permute-done | bytes 135200 | tf_op jit(solution)/shard_map/ppermute | solution.py:285
  37.8 1.2 %collective-permute-done.1.rows2_ref = f32[264,128]{1,0:T(8,128)S(1)} collective-permute-done((f32[264,128]{1,0:T(8,128)S(1)}, f32[264,128]{1,0:T(8,128)S(1)}, u32[]{:S(2)}, u32[]{:S(2)}) %collective-permute-start.1) | collective-permute-done | bytes 135200 | tf_op jit(solution)/shard_map/ppermute | solution.py:285
  39.0 0.6 collective-permute-done.rows1_ref
  39.6 2.4 %shard_map.81 = (f32[1024,1024]{1,0:T(8,128)S(1)}, f32[32,8,128]{2,1,0:T(8,128)S(1)}) custom-call(f32[264,128]{1,0:T(8,128)S(1)} %collective-permute-done.rows1_ref, f32[264,128]{1,0:T(8,128)S(1)} %collective-permute-done.1.rows2_ref, f32[264,128]{1,0:T(8,128)S(1)} %collective-permute-done.2.rows3_ref, bf16[896,1024]{1,0:T(8,128)(2,1)S(1)} %get-tuple-element.22.b_ref, ...), custom_call_target="tpu_custom_call" | custom-call | tf_op jit(solution)/shard_map/pallas_call | solution.py:297
  42.0 10.0 %all_to_all.25.parts_ref = f32[32,8,128]{2,1,0:T(8,128)S(1)} all-to-all(f32[32,8,128]{2,1,0:T(8,128)S(1)} %get-tuple-element.26), channel_id=1, replica_groups={{77,76,79,78,73,72,75,74,69,68,71,70,65,64,67,66,13,12,15,14,9,8,11,10,..., dimensions={0} | all-to-all | bytes 262144 | tf_op jit(solution)/shard_map/all_to_all | solution.py:303
  52.0 1.0 %shard_map.82 = f32[16,8,128]{2,1,0:T(8,128)S(1)} custom-call(f32[32,8,128]{2,1,0:T(8,128)S(1)} %all_to_all.25.parts_ref, f32[1024,1024]{1,0:T(8,128)S(1)} %get-tuple-element.27.cost_ref), custom_call_target="tpu_custom_call" | custom-call | tf_op jit(solution)/shard_map/pallas_call | solution.py:304
  53.0 14.7 %all_to_all.26.parts_ref = f32[16,8,128]{2,1,0:T(8,128)S(1)} all-to-all(f32[16,8,128]{2,1,0:T(8,128)S(1)} %shard_map.82), channel_id=1, replica_groups={{288,304,256,272,416,432,384,400,32,48,0,16,160,176,128,144},{289,305,2..., dimensions={0} | all-to-all | bytes 131072 | tf_op jit(solution)/shard_map/all_to_all | solution.py:305
  67.8 0.9 shard_map.83
  68.7 9.6 %all_to_all.27.parts_ref = f32[32,8,128]{2,1,0:T(8,128)S(1)} all-to-all(f32[32,8,128]{2,1,0:T(8,128)S(1)} %shard_map.83), channel_id=1, replica_groups={{77,76,79,78,73,72,75,74,69,68,71,70,65,64,67,66,13,12,15,14,9,8,11,10,..., dimensions={0} | all-to-all | bytes 262144 | tf_op jit(solution)/shard_map/all_to_all | solution.py:307
  78.2 1.1 %shard_map.84 = (f32[64,1,1152]{2,1,0:T(1,128)S(1)}, f32[8,128]{1,0:T(8,128)S(1)}) custom-call(f32[32,8,128]{2,1,0:T(8,128)S(1)} %all_to_all.27.parts_ref, f32[1024,1024]{1,0:T(8,128)S(1)} %get-tuple-element.27.cost_ref), custom_call_target="tpu_custom_call" | custom-call | tf_op jit(solution)/shard_map/pallas_call | solution.py:308
  79.3 21.1 %all_to_all.28.parts_ref = f32[64,1,1152]{2,1,0:T(1,128)S(1)} all-to-all(f32[64,1,1152]{2,1,0:T(1,128)S(1)} %get-tuple-element.28), channel_id=1, replica_groups={{288,296,304,312,256,264,272,280,352,360,368,376,320,328,336,344,416,42..., dimensions={0} | all-to-all | bytes 589824 | tf_op jit(solution)/shard_map/all_to_all | solution.py:311
  100.4 0.7 shard_map.85
Async XLA Ops:
  2.2 33.0 %all-to-all-start = ((f32[64,16,128]{2,1,0:T(8,128)}), f32[64,16,128]{2,1,0:T(8,128)S(1)}, u32[]{:S(2)}, u32[]{:S(2)}) async-start(f32[64,16,128]{2,1,0:T(8,128)} %shard_map.77), calls=%async_computation | async-start | bytes 1048576 | tf_op jit(solution)/shard_map/all_to_all | solution.py:284
  22.9 14.9 %collective-permute-start.2 = (f32[264,128]{1,0:T(8,128)S(1)}, f32[264,128]{1,0:T(8,128)S(1)}, u32[]{:S(2)}, u32[]{:S(2)}) collective-permute-start(f32[264,128]{1,0:T(8,128)S(1)} %shard_map.78.rows_ref), channel_id=1, source_target_pairs={{0,72},{8,64},{64,8},{72,0},{1,73},{9,65},{65,9},{73,1},{2,74},{10... | collective-permute-start | bytes 405512 | tf_op jit(solution)/shard_map/ppermute | solution.py:285
  26.3 12.6 %collective-permute-start.1 = (f32[264,128]{1,0:T(8,128)S(1)}, f32[264,128]{1,0:T(8,128)S(1)}, u32[]{:S(2)}, u32[]{:S(2)}) collective-permute-start(f32[264,128]{1,0:T(8,128)S(1)} %shard_map.78.rows_ref), channel_id=1, source_target_pairs={{0,64},{8,72},{64,0},{72,8},{1,65},{9,73},{65,1},{73,9},{2,66},{10... | collective-permute-start | bytes 405512 | tf_op jit(solution)/shard_map/ppermute | solution.py:285
  29.6 9.9 %collective-permute-start = (f32[264,128]{1,0:T(8,128)S(1)}, f32[264,128]{1,0:T(8,128)S(1)}, u32[]{:S(2)}, u32[]{:S(2)}) collective-permute-start(f32[264,128]{1,0:T(8,128)S(1)} %shard_map.78.rows_ref), channel_id=1, source_target_pairs={{0,8},{8,0},{64,72},{72,64},{1,9},{9,1},{65,73},{73,65},{2,10},{10... | collective-permute-start | bytes 405512 | tf_op jit(solution)/shard_map/ppermute | solution.py:285
  32.1 0.7 copy-start
  32.8 0.7 copy-start.1

commit v5 on v4

--- a/solution.py
+++ b/solution.py
@@ -138,7 +138,7 @@
     return top + jnp.log2(jnp.sum(jnp.exp2(flat - top), axis=0, keepdims=True))
 
 
-def group_costs(rows_ref, group, b, squares_v, cost_ref, part_ref, piece_ref):
+def left_rows(rows_ref):
     x = rows_ref[0:OWN, :]
     squares = jnp.sum(x * x, axis=1, keepdims=True) * (-SCALE / T)
     hi, mid, low = split3(x * (2.0 * SCALE / T))
@@ -146,18 +146,25 @@
     flat = [jnp.broadcast_to(rows_ref[OWN + k : OWN + k + 1, :], (T, T)).T for k in range(OWN // T)]
     label = jnp.concatenate(flat, axis=0).astype(jnp.int32)
     ext = jnp.where((lane % 16 == label) & (lane < 48), 1.0, 0.0).astype(BF16)
-    a = jnp.concatenate([hi, hi, mid, hi, low, mid, ext], axis=1)
-    start = pl.multiple_of(group * OWN, OWN)
-    cost_ref[pl.ds(start, OWN), :] = jnp.dot(a, b, preferred_element_type=F32) + squares + squares_v
+    return jnp.concatenate([hi, hi, mid, hi, low, mid, ext], axis=1), squares
+
+
+def group_costs(left, b, squares_v, cost_ref, start):
+    a, squares = left
+    cost_ref[start : start + OWN, :] = jnp.dot(a, b, preferred_element_type=F32) + squares + squares_v
+
+
+def group_lse(cost_ref, start, place, part_ref, piece_ref):
     for half in range(OWN // T):
 
         def load(block, row):
-            return cost_ref[pl.ds(start + half * T + row, 32), block * T : (block + 1) * T]
-
-        part_ref[pl.ds(group * 2 + half, 1), :] = rows_block(load, piece_ref.at[half])
-
-
-def own_costs_kernel(rows_ref, val_ref, kinds_ref, cost_ref, part_ref, b_ref, squares_ref, piece_ref):
+            first = start + half * T + row
+            return cost_ref[first : first + 32, block * T : (block + 1) * T]
+
+        part_ref[pl.ds(place + half, 1), :] = rows_block(load, piece_ref.at[half])
+
+
+def first_costs_kernel(rows_ref, rows3_ref, val_ref, kinds_ref, quarter_ref, cost_ref, part_ref, b_ref, squares_ref, piece_ref):
     for block in range(NB):
         lanes = slice(block * T, (block + 1) * T)
         y = in_order(val_ref[pl.ds(block, T, stride=NB), :])
@@ -166,42 +173,60 @@
             b_ref[k * T : (k + 1) * T, lanes] = part
         squares_ref[:, lanes] = jnp.broadcast_to(jnp.sum(y * y, axis=0, keepdims=True) * (-SCALE / T), (8, T))
     b_ref[6 * T : 7 * T, :] = kinds_ref[...]
-    group_costs(rows_ref, 0, b_ref[...], squares_ref[0:1, :], cost_ref, part_ref, piece_ref)
+    tile_costs((rows_ref, rows3_ref), (0, 3), quarter_ref[0], b_ref, squares_ref, cost_ref, part_ref, piece_ref)
 
 
 def other_costs_kernel(
-    rows1_ref, rows2_ref, rows3_ref, b_ref, squares_ref, quarter_ref, own_ref, part_ref, cost_ref, out_ref, full_ref, piece_ref
+    rows1_ref, rows2_ref, b_ref, squares_ref, quarter_ref, part_ref, cost_ref, out_ref, full_ref, piece_ref
 ):
-    quarter = quarter_ref[0]
-    full_ref[pl.ds(quarter * 2, 2), :] = part_ref[0:2, :]
-    cost_ref[pl.ds(pl.multiple_of(quarter * OWN, OWN), OWN), :] = own_ref[...]
-    for apart, rows_ref in enumerate((rows1_ref, rows2_ref, rows3_ref)):
-        group = quarter ^ (apart + 1)
-        group_costs(rows_ref, group, b_ref[...], squares_ref[0:1, :], cost_ref, full_ref, piece_ref.at[apart])
+    full_ref[...] = part_ref[...]
+    tile_costs((rows1_ref, rows2_ref), (1, 2), quarter_ref[0], b_ref, squares_ref, cost_ref, full_ref, piece_ref)
     send(full_ref, out_ref)
 
 
-def rows_step_kernel(parts_ref, cost_ref, out_ref, piece_ref, part_ref):
+def tile_costs(groups, aparts, quarter, b_ref, squares_ref, cost_ref, part_ref, piece_ref):
+    for k, rows_ref in enumerate(groups):
+        group_costs(left_rows(rows_ref), b_ref[...], squares_ref[0:1, :], cost_ref, k * OWN)
+    for k, apart in enumerate(aparts):
+        group_lse(cost_ref, k * OWN, (quarter ^ apart) * 2, part_ref, piece_ref.at[k])
+
+
+def tile_rows(first_ref, rest_ref, s):
+    return (first_ref, s * T) if s < NB // 2 else (rest_ref, (s - NB // 2) * T)
+
+
+def place(quarter, s):
+    return (quarter ^ (0, 3, 1, 2)[s // 2]) * 2 + s % 2
+
+
+def rows_step_kernel(parts_ref, first_ref, rest_ref, quarter_ref, out_ref, piece_ref, part_ref):
     g = -15.0 - lse_lead(parts_ref)
     wide = [jnp.broadcast_to(g[block : block + 1], (32, T)) for block in range(NB)]
     for s in range(NB):
+        cost_ref, start = tile_rows(first_ref, rest_ref, s)
 
         def load(block, row):
-            return cost_ref[s * T + row : s * T + row + 32, block * T : (block + 1) * T] + wide[block]
-
-        part_ref[s : s + 1, :] = rows_block(load, piece_ref.at[s])
+            return cost_ref[start + row : start + row + 32, block * T : (block + 1) * T] + wide[block]
+
+        part_ref[pl.ds(place(quarter_ref[0], s), 1), :] = rows_block(load, piece_ref.at[s])
     send(part_ref, out_ref)
 
 
-def columns_lse(f, cost_ref, wide_ref, part_ref):
+def columns_lse(f_ref, first_ref, rest_ref, quarter, wide_ref, part_ref):
     for s in range(NB):
-        wide_ref[s * T : (s + 1) * T, :] = jnp.broadcast_to(f[s : s + 1], (T, T)).T
+        row = f_ref[pl.ds(place(quarter, s), 1), :]
+        wide_ref[s * T : (s + 1) * T, :] = jnp.broadcast_to(row, (T, T)).T
     for block in range(NB):
         lanes = slice(block * T, (block + 1) * T)
         tops, totals = [], []
-        for start in range(0, SIDE, 64):
-            rows = [slice(start + 8 * j, start + 8 * j + 8) for j in range(8)]
-            top, total = lse_list([cost_ref[r, lanes] + wide_ref[r, :] for r in rows])
+        for chunk in range(SIDE // 64):
+            cost_ref, first = tile_rows(first_ref, rest_ref, chunk // 2)
+            first = first + chunk % 2 * 64
+            zs = []
+            for j in range(0, 64, 8):
+                at = chunk * 64 + j
+                zs.append(cost_ref[first + j : first + j + 8, lanes] + wide_ref[at : at + 8, :])
+            top, total = lse_list(zs)
             tops.append(top)
             totals.append(total)
         best = jnp.max(tree(jnp.maximum, tops), axis=0, keepdims=True)
@@ -209,16 +234,16 @@
         part_ref[block : block + 1, :] = best + jnp.log2(jnp.sum(total, axis=0, keepdims=True))
 
 
-def columns_step_kernel(parts_ref, cost_ref, out_ref, wide_ref, part_ref):
-    f = -14.0 - lse_lead(parts_ref)
-    columns_lse(f, cost_ref, wide_ref, part_ref)
+def columns_step_kernel(parts_ref, first_ref, rest_ref, quarter_ref, out_ref, wide_ref, part_ref, f_ref):
+    f_ref[...] = -14.0 - lse_lead(parts_ref)
+    columns_lse(f_ref, first_ref, rest_ref, quarter_ref[0], wide_ref, part_ref)
     send(part_ref, out_ref)
 
 
-def last_columns_kernel(parts_ref, cost_ref, out_ref, f_ref, wide_ref, part_ref, row_ref):
+def last_columns_kernel(parts_ref, first_ref, rest_ref, quarter_ref, out_ref, f_ref, wide_ref, part_ref, row_ref):
     f = -14.0 - lse_lead(parts_ref)
     f_ref[...] = f
-    columns_lse(f, cost_ref, wide_ref, part_ref)
+    columns_lse(f_ref, first_ref, rest_ref, quarter_ref[0], wide_ref, part_ref)
     for block in range(NB):
         row_ref[:, block * T : (block + 1) * T] = part_ref[block : block + 1, :]
     row_ref[:, SIDE : SIDE + T] = jnp.sum(f, axis=0, keepdims=True)
@@ -288,26 +313,27 @@
         quarter, val_labels.reshape(32, T), class_cost
     )
     part, piece, wide = vmem((NB, T)), vmem((NB, T, T)), vmem((SIDE, T))
-    own, part_own, b, squares = call(
-        own_costs_kernel,
-        [shape((OWN, SIDE)), shape((NB, T)), shape((7 * T, SIDE), BF16), shape((8, SIDE))],
-        [SPEC] * 3,
-        [vmem((2, T, T))],
-    )(rows, columns.reshape(SIDE, T), kinds)
-    cost, parts = call(
+    first, part_first, b, squares = call(
+        first_costs_kernel,
+        [shape((2 * OWN, SIDE)), shape((NB, T)), shape((7 * T, SIDE), BF16), shape((8, SIDE))],
+        [SPEC] * 4 + [SCALARS],
+        [vmem((2, 2, T, T))],
+    )(rows, others[2], columns.reshape(SIDE, T), kinds, quarter)
+    rest, parts = call(
         other_costs_kernel,
-        [shape((SIDE, SIDE)), shape((32, NB, T))],
-        [SPEC] * 5 + [SCALARS] + [SPEC] * 2,
-        [part, vmem((3, 2, T, T))],
-    )(*others, b, squares, quarter, own, part_own)
+        [shape((2 * OWN, SIDE)), shape((32, NB, T))],
+        [SPEC] * 4 + [SCALARS, SPEC],
+        [part, vmem((2, 2, T, T))],
+    )(*others[:2], b, squares, quarter, part_first)
+    step = [SPEC] * 3 + [SCALARS]
     parts = lax.all_to_all(parts, ALONG, 0, 0, axis_index_groups=ALONG_ORDER)
-    (parts,) = call(columns_step_kernel, [shape((16, NB, T))], [SPEC] * 2, [wide, part])(parts, cost)
+    (parts,) = call(columns_step_kernel, [shape((16, NB, T))], step, [wide, part, part])(parts, first, rest, quarter)
     parts = lax.all_to_all(parts, ACROSS, 0, 0, axis_index_groups=ACROSS_ORDER)
-    (parts,) = call(rows_step_kernel, [shape((32, NB, T))], [SPEC] * 2, [piece, part])(parts, cost)
+    (parts,) = call(rows_step_kernel, [shape((32, NB, T))], step, [piece, part])(parts, first, rest, quarter)
     parts = lax.all_to_all(parts, ALONG, 0, 0, axis_index_groups=ALONG_ORDER)
     parts, f = call(
-        last_columns_kernel, [shape((64, 1, SIDE + T)), shape((NB, T))], [SPEC] * 2, [wide, part, vmem((1, SIDE + T))]
-    )(parts, cost)
+        last_columns_kernel, [shape((64, 1, SIDE + T)), shape((NB, T))], step, [wide, part, vmem((1, SIDE + T))]
+    )(parts, first, rest, quarter)
     parts = lax.all_to_all(parts, ROW, 0, 0, axis_index_groups=ROW_ORDER)
     value, potential = call(finish_kernel, [shape((2, T)), shape((4, 1, SIDE))], [SPEC, SPEC, SCALARS])(parts, f, quarter)
     return value.reshape(256), potential.reshape(4096)

time: 102 us -> 101 us (level)
  local copies, waits for them, and re-layouts: 1.41 us -> 0.01 us
    ppermute x3, waiting for transfers between devices: 3.14 us -> 5.4 us  [local(): lax.ppermute(rows, QUAD, [(i, i ^ apart) for i in range(4)])]
    all_to_all x1, waiting for transfers between devices: 1.46 us -> 0.01 us  [local(): columns = lax.all_to_all(columns, ROW, 0, 0, axis_index_groups=ROW_ORDER)]
    unnamed x4, local copies, waits for them, and re-layouts: 1.41 us -> 0.01 us
  transfers between devices with their start and end apart: 4 -> 4, of which waited for: 4 -> 1; matrix products, arithmetic and copies ran while one was open for 0% -> 0% of each run, Pallas kernels for 3% -> 4%
where the time goes in v5:
time: 101 us; the launch traced here: 100 us
  blocking collectives  55.4 us (55%)
  starting transfers between devices  28.1 us (28%)
  Pallas kernels  10.7 us (11%)
  waiting for transfers between devices  5.41 us (5%)
    all_to_all x1, blocking collectives, local(): parts = lax.all_to_all(parts, ROW, 0, 0, axis_index_groups=ROW_ORDER)  21.1 us
    all_to_all x2, blocking collectives, local(): parts = lax.all_to_all(parts, ALONG, 0, 0, axis_index_groups=ALONG_ORDER)  19.5 us
    all_to_all x1, starting transfers between devices, local(): columns = lax.all_to_all(columns, ROW, 0, 0, axis_index_groups=ROW_ORDER)  18.9 us
    all_to_all x1, blocking collectives, local(): parts = lax.all_to_all(parts, ACROSS, 0, 0, axis_index_groups=ACROSS_ORDER)  14.7 us
    ppermute x3, starting transfers between devices, local(): lax.ppermute(rows, QUAD, [(i, i ^ apart) for i in range(4)])  9.21 us
    ppermute x3, waiting for transfers between devices, local(): lax.ppermute(rows, QUAD, [(i, i ^ apart) for i in range(4)])  5.4 us
  transfers between devices with their start and end apart: 4, of which 1 were waited for; matrix products, arithmetic and copies ran while one was open for 0% of the time, Pallas kernels for 4%

profile of v5, /device:TPU:8, one launch (start us, length us, event | category | flops | bytes accessed | tf_op | source)
XLA Modules:
  0.0 100.4 jit_solution(13008968932359814466)
XLA Ops:
  0.6 0.0 copy-start.1
  0.6 0.0 copy-start
  0.7 1.6 %shard_map.77 = f32[64,16,128]{2,1,0:T(8,128)} custom-call(f32[2,4096]{1,0:T(2,128)} %bitcast.8), custom_call_target="tpu_custom_call" | custom-call | tf_op jit(solution)/shard_map/pallas_call | solution.py:293
  2.3 18.9 %all-to-all-start = ((f32[64,16,128]{2,1,0:T(8,128)}), f32[64,16,128]{2,1,0:T(8,128)S(1)}, u32[]{:S(2)}, u32[]{:S(2)}) async-start(f32[64,16,128]{2,1,0:T(8,128)} %shard_map.77), calls=%async_computation | async-start | bytes 1048576 | tf_op jit(solution)/shard_map/all_to_all | solution.py:309
  21.2 1.7 %shard_map.78.rows_ref = f32[264,128]{1,0:T(8,128)S(1)} custom-call(s32[256]{0:T(256)} %index_hbm, s32[2048]{0:T(1024)} %labels_hbm.1, f32[2048,128]{1,0:T(8,128)} %pool_hbm.1), custom_call_target="tpu_custom_call" | custom-call | tf_op jit(solution)/shard_map/pallas_call | solution.py:297
  22.9 3.4 %collective-permute-start.2 = (f32[264,128]{1,0:T(8,128)S(1)}, f32[264,128]{1,0:T(8,128)S(1)}, u32[]{:S(2)}, u32[]{:S(2)}) collective-permute-start(f32[264,128]{1,0:T(8,128)S(1)} %shard_map.78.rows_ref), channel_id=1, source_target_pairs={{0,72},{8,64},{64,8},{72,0},{1,73},{9,65},{65,9},{73,1},{2,74},{10... | collective-permute-start | bytes 405512 | tf_op jit(solution)/shard_map/ppermute | solution.py:310
  26.3 3.3 %collective-permute-start.1 = (f32[264,128]{1,0:T(8,128)S(1)}, f32[264,128]{1,0:T(8,128)S(1)}, u32[]{:S(2)}, u32[]{:S(2)}) collective-permute-start(f32[264,128]{1,0:T(8,128)S(1)} %shard_map.78.rows_ref), channel_id=1, source_target_pairs={{0,64},{8,72},{64,0},{72,8},{1,65},{9,73},{65,1},{73,9},{2,66},{10... | collective-permute-start | bytes 405512 | tf_op jit(solution)/shard_map/ppermute | solution.py:310
  29.7 2.5 %collective-permute-start = (f32[264,128]{1,0:T(8,128)S(1)}, f32[264,128]{1,0:T(8,128)S(1)}, u32[]{:S(2)}, u32[]{:S(2)}) collective-permute-start(f32[264,128]{1,0:T(8,128)S(1)} %shard_map.78.rows_ref), channel_id=1, source_target_pairs={{0,8},{8,0},{64,72},{72,64},{1,9},{9,1},{65,73},{73,65},{2,10},{10... | collective-permute-start | bytes 405512 | tf_op jit(solution)/shard_map/ppermute | solution.py:310
  32.2 0.0 copy-done.1
  32.2 0.0 copy-done
  32.2 0.2 shard_map.79.kinds_ref
  32.4 5.4 %collective-permute-done.2.rows3_ref = f32[264,128]{1,0:T(8,128)S(1)} collective-permute-done((f32[264,128]{1,0:T(8,128)S(1)}, f32[264,128]{1,0:T(8,128)S(1)}, u32[]{:S(2)}, u32[]{:S(2)}) %collective-permute-start.2) | collective-permute-done | bytes 135200 | tf_op jit(solution)/shard_map/ppermute | solution.py:310
  37.8 0.0 all-to-all-done
  37.8 1.9 %shard_map.80 = (f32[512,1024]{1,0:T(8,128)S(1)}, f32[8,128]{1,0:T(8,128)S(1)}, bf16[896,1024]{1,0:T(8,128)(2,1)S(1)}, f32[8,1024]{1,0:T(8,128)S(1)}) custom-call(f32[264,128]{1,0:T(8,128)S(1)} %shard_map.78.rows_ref, f32[264,128]{1,0:T(8,128)S(1)} %collective-permute-done.2.rows3_ref, f32[1024,128]{1,0:T(8,128)S(1)} %bitcast.6, ...), custom_call_target="tpu_custom_call" | custom-call | tf_op jit(solution)/shard_map/pallas_call | solution.py:316
  39.7 0.0 collective-permute-done.1.rows2_ref
  39.7 0.0 collective-permute-done.rows1_ref
  39.7 1.7 %shard_map.81 = (f32[512,1024]{1,0:T(8,128)S(1)}, f32[32,8,128]{2,1,0:T(8,128)S(1)}) custom-call(f32[264,128]{1,0:T(8,128)S(1)} %collective-permute-done.rows1_ref, f32[264,128]{1,0:T(8,128)S(1)} %collective-permute-done.1.rows2_ref, bf16[896,1024]{1,0:T(8,128)(2,1)S(1)} %get-tuple-element.22.b_ref, f32[8,1024]{1,0:T(8,128)S(1)} %get-tuple-element.23.squares_ref, ...), custom_call_target="tpu_custom_call" | custom-call | tf_op jit(solution)/shard_map/pallas_call | solution.py:322
  41.4 10.0 %all_to_all.25.parts_ref = f32[32,8,128]{2,1,0:T(8,128)S(1)} all-to-all(f32[32,8,128]{2,1,0:T(8,128)S(1)} %get-tuple-element.25), channel_id=1, replica_groups={{77,76,79,78,73,72,75,74,69,68,71,70,65,64,67,66,13,12,15,14,9,8,11,10,..., dimensions={0} | all-to-all | bytes 262144 | tf_op jit(solution)/shard_map/all_to_all | solution.py:329
  51.4 1.0 shard_map.82
  52.4 14.7 %all_to_all.26.parts_ref = f32[16,8,128]{2,1,0:T(8,128)S(1)} all-to-all(f32[16,8,128]{2,1,0:T(8,128)S(1)} %shard_map.82), channel_id=1, replica_groups={{288,304,256,272,416,432,384,400,32,48,0,16,160,176,128,144},{289,305,2..., dimensions={0} | all-to-all | bytes 131072 | tf_op jit(solution)/shard_map/all_to_all | solution.py:331
  67.1 0.9 shard_map.83
  68.0 9.6 %all_to_all.27.parts_ref = f32[32,8,128]{2,1,0:T(8,128)S(1)} all-to-all(f32[32,8,128]{2,1,0:T(8,128)S(1)} %shard_map.83), channel_id=1, replica_groups={{77,76,79,78,73,72,75,74,69,68,71,70,65,64,67,66,13,12,15,14,9,8,11,10,..., dimensions={0} | all-to-all | bytes 262144 | tf_op jit(solution)/shard_map/all_to_all | solution.py:333
  77.5 1.0 %shard_map.84 = (f32[64,1,1152]{2,1,0:T(1,128)S(1)}, f32[8,128]{1,0:T(8,128)S(1)}) custom-call(f32[32,8,128]{2,1,0:T(8,128)S(1)} %all_to_all.27.parts_ref, f32[512,1024]{1,0:T(8,128)S(1)} %get-tuple-element.26.first_ref, f32[512,1024]{1,0:T(8,128)S(1)} %get-tuple-element.27.rest_ref, s32[1]{0:T(128)} %bitcast.2.quarter_ref), custom_call_target="tpu_custom_call" | custom-call | tf_op jit(solution)/shard_map/pallas_call | solution.py:334
  78.6 21.1 %all_to_all.28.parts_ref = f32[64,1,1152]{2,1,0:T(1,128)S(1)} all-to-all(f32[64,1,1152]{2,1,0:T(1,128)S(1)} %get-tuple-element.28), channel_id=1, replica_groups={{288,296,304,312,256,264,272,280,352,360,368,376,320,328,336,344,416,42..., dimensions={0} | all-to-all | bytes 589824 | tf_op jit(solution)/shard_map/all_to_all | solution.py:337
  99.7 0.7 shard_map.85
Async XLA Ops:
  0.6 31.5 %copy-start.1 = (f32[10,10]{1,0:T(8,128)S(1)}, f32[10,10]{1,0:T(8,128)}, u32[]{:S(2)}) copy-start(f32[10,10]{1,0:T(8,128)} %class_ref) | copy-start | bytes 1204
  0.6 31.5 %copy-start = (s32[4096]{0:T(1024)S(1)}, s32[4096]{0:T(1024)}, u32[]{:S(2)}) copy-start(s32[4096]{0:T(1024)} %param.10) | copy-start | bytes 49156
  2.3 35.5 %all-to-all-start = ((f32[64,16,128]{2,1,0:T(8,128)}), f32[64,16,128]{2,1,0:T(8,128)S(1)}, u32[]{:S(2)}, u32[]{:S(2)}) async-start(f32[64,16,128]{2,1,0:T(8,128)} %shard_map.77), calls=%async_computation | async-start | bytes 1048576 | tf_op jit(solution)/shard_map/all_to_all | solution.py:309
  22.9 14.9 %collective-permute-start.2 = (f32[264,128]{1,0:T(8,128)S(1)}, f32[264,128]{1,0:T(8,128)S(1)}, u32[]{:S(2)}, u32[]{:S(2)}) collective-permute-start(f32[264,128]{1,0:T(8,128)S(1)} %shard_map.78.rows_ref), channel_id=1, source_target_pairs={{0,72},{8,64},{64,8},{72,0},{1,73},{9,65},{65,9},{73,1},{2,74},{10... | collective-permute-start | bytes 405512 | tf_op jit(solution)/shard_map/ppermute | solution.py:310
  26.3 13.4 %collective-permute-start.1 = (f32[264,128]{1,0:T(8,128)S(1)}, f32[264,128]{1,0:T(8,128)S(1)}, u32[]{:S(2)}, u32[]{:S(2)}) collective-permute-start(f32[264,128]{1,0:T(8,128)S(1)} %shard_map.78.rows_ref), channel_id=1, source_target_pairs={{0,64},{8,72},{64,0},{72,8},{1,65},{9,73},{65,1},{73,9},{2,66},{10... | collective-permute-start | bytes 405512 | tf_op jit(solution)/shard_map/ppermute | solution.py:310
  29.7 10.1 %collective-permute-start = (f32[264,128]{1,0:T(8,128)S(1)}, f32[264,128]{1,0:T(8,128)S(1)}, u32[]{:S(2)}, u32[]{:S(2)}) collective-permute-start(f32[264,128]{1,0:T(8,128)S(1)} %shard_map.78.rows_ref), channel_id=1, source_target_pairs={{0,8},{8,0},{64,72},{72,64},{1,9},{9,1},{65,73},{73,65},{2,10},{10... | collective-permute-start | bytes 405512 | tf_op jit(solution)/shard_map/ppermute | solution.py:310

commit v6 on v5

--- a/solution.py
+++ b/solution.py
@@ -149,6 +149,13 @@
     return jnp.concatenate([hi, hi, mid, hi, low, mid, ext], axis=1), squares
 
 
+def left_kernel(rows_ref, rows1_ref, left_ref, squares_ref):
+    for k, ref in enumerate((rows_ref, rows1_ref)):
+        a, squares = left_rows(ref)
+        left_ref[k * OWN : (k + 1) * OWN, :] = a
+        squares_ref[k * OWN : (k + 1) * OWN, :] = jnp.broadcast_to(squares, (OWN, T))
+
+
 def group_costs(left, b, squares_v, cost_ref, start):
     a, squares = left
     cost_ref[start : start + OWN, :] = jnp.dot(a, b, preferred_element_type=F32) + squares + squares_v
@@ -164,7 +171,7 @@
         part_ref[pl.ds(place + half, 1), :] = rows_block(load, piece_ref.at[half])
 
 
-def first_costs_kernel(rows_ref, rows3_ref, val_ref, kinds_ref, quarter_ref, cost_ref, part_ref, b_ref, squares_ref, piece_ref):
+def first_costs_kernel(left_ref, left_squares_ref, val_ref, kinds_ref, quarter_ref, cost_ref, part_ref, b_ref, squares_ref, piece_ref):
     for block in range(NB):
         lanes = slice(block * T, (block + 1) * T)
         y = in_order(val_ref[pl.ds(block, T, stride=NB), :])
@@ -173,20 +180,21 @@
             b_ref[k * T : (k + 1) * T, lanes] = part
         squares_ref[:, lanes] = jnp.broadcast_to(jnp.sum(y * y, axis=0, keepdims=True) * (-SCALE / T), (8, T))
     b_ref[6 * T : 7 * T, :] = kinds_ref[...]
-    tile_costs((rows_ref, rows3_ref), (0, 3), quarter_ref[0], b_ref, squares_ref, cost_ref, part_ref, piece_ref)
+    lefts = [(left_ref[rows, :], left_squares_ref[rows, 0:1]) for rows in (slice(0, OWN), slice(OWN, 2 * OWN))]
+    tile_costs(lefts, (0, 1), quarter_ref[0], b_ref, squares_ref, cost_ref, part_ref, piece_ref)
 
 
 def other_costs_kernel(
-    rows1_ref, rows2_ref, b_ref, squares_ref, quarter_ref, part_ref, cost_ref, out_ref, full_ref, piece_ref
+    rows2_ref, rows3_ref, b_ref, squares_ref, quarter_ref, part_ref, cost_ref, out_ref, full_ref, piece_ref
 ):
     full_ref[...] = part_ref[...]
-    tile_costs((rows1_ref, rows2_ref), (1, 2), quarter_ref[0], b_ref, squares_ref, cost_ref, full_ref, piece_ref)
+    tile_costs((left_rows(rows2_ref), left_rows(rows3_ref)), (2, 3), quarter_ref[0], b_ref, squares_ref, cost_ref, full_ref, piece_ref)
     send(full_ref, out_ref)
 
 
-def tile_costs(groups, aparts, quarter, b_ref, squares_ref, cost_ref, part_ref, piece_ref):
-    for k, rows_ref in enumerate(groups):
-        group_costs(left_rows(rows_ref), b_ref[...], squares_ref[0:1, :], cost_ref, k * OWN)
+def tile_costs(lefts, aparts, quarter, b_ref, squares_ref, cost_ref, part_ref, piece_ref):
+    for k, left in enumerate(lefts):
+        group_costs(left, b_ref[...], squares_ref[0:1, :], cost_ref, k * OWN)
     for k, apart in enumerate(aparts):
         group_lse(cost_ref, k * OWN, (quarter ^ apart) * 2, part_ref, piece_ref.at[k])
 
@@ -196,7 +204,7 @@
 
 
 def place(quarter, s):
-    return (quarter ^ (0, 3, 1, 2)[s // 2]) * 2 + s % 2
+    return (quarter ^ (s // 2)) * 2 + s % 2
 
 
 def rows_step_kernel(parts_ref, first_ref, rest_ref, quarter_ref, out_ref, piece_ref, part_ref):
@@ -307,24 +315,25 @@
         ],
     )(far(window_index), far(pool_labels), far(pool))
     columns = lax.all_to_all(columns, ROW, 0, 0, axis_index_groups=ROW_ORDER)
-    others = [lax.ppermute(rows, QUAD, [(i, i ^ apart) for i in range(4)]) for apart in (1, 2, 3)]
+    others = {apart: lax.ppermute(rows, QUAD, [(i, i ^ apart) for i in range(4)]) for apart in (2, 3, 1)}
     rows, val_labels, class_cost = lax.optimization_barrier((rows, val_labels, class_cost))
     (kinds,) = call(labels_kernel, [shape((T, SIDE), BF16)], [SCALARS, SPEC, SPEC])(
         quarter, val_labels.reshape(32, T), class_cost
     )
     part, piece, wide = vmem((NB, T)), vmem((NB, T, T)), vmem((SIDE, T))
+    left, left_squares = call(left_kernel, [shape((2 * OWN, 7 * T), BF16), shape((2 * OWN, T))], [SPEC] * 2)(rows, others[1])
     first, part_first, b, squares = call(
         first_costs_kernel,
         [shape((2 * OWN, SIDE)), shape((NB, T)), shape((7 * T, SIDE), BF16), shape((8, SIDE))],
         [SPEC] * 4 + [SCALARS],
         [vmem((2, 2, T, T))],
-    )(rows, others[2], columns.reshape(SIDE, T), kinds, quarter)
+    )(left, left_squares, columns.reshape(SIDE, T), kinds, quarter)
     rest, parts = call(
         other_costs_kernel,
         [shape((2 * OWN, SIDE)), shape((32, NB, T))],
         [SPEC] * 4 + [SCALARS, SPEC],
         [part, vmem((2, 2, T, T))],
-    )(*others[:2], b, squares, quarter, part_first)
+    )(others[2], others[3], b, squares, quarter, part_first)
     step = [SPEC] * 3 + [SCALARS]
     parts = lax.all_to_all(parts, ALONG, 0, 0, axis_index_groups=ALONG_ORDER)
     (parts,) = call(columns_step_kernel, [shape((16, NB, T))], step, [wide, part, part])(parts, first, rest, quarter)

time: 101 us -> 101 us (level)
  no operation moved by 1% of the time
where the time goes in v6:
time: 101 us
  blocking collectives  55.5 us (55%)
  starting transfers between devices  28.1 us (28%)
  Pallas kernels  11.1 us (11%)
  waiting for transfers between devices  5.17 us (5%)
    all_to_all x1, blocking collectives, local(): parts = lax.all_to_all(parts, ROW, 0, 0, axis_index_groups=ROW_ORDER)  21.1 us
    all_to_all x2, blocking collectives, local(): parts = lax.all_to_all(parts, ALONG, 0, 0, axis_index_groups=ALONG_ORDER)  19.6 us
    all_to_all x1, starting transfers between devices, local(): columns = lax.all_to_all(columns, ROW, 0, 0, axis_index_groups=ROW_ORDER)  18.9 us
    all_to_all x1, blocking collectives, local(): parts = lax.all_to_all(parts, ACROSS, 0, 0, axis_index_groups=ACROSS_ORDER)  14.7 us
    ppermute x3, starting transfers between devices, local(): lax.ppermute(rows, QUAD, [(i, i ^ apart) for i in range(4)])  9.21 us
    ppermute x3, waiting for transfers between devices, local(): lax.ppermute(rows, QUAD, [(i, i ^ apart) for i in range(4)])  5.17 us
  transfers between devices with their start and end apart: 4, of which 1 were waited for; matrix products, arithmetic and copies ran while one was open for 0% of the time, Pallas kernels for 4%

profile of v6, /device:TPU:8, one launch (start us, length us, event | category | flops | bytes accessed | tf_op | source)
XLA Modules:
  0.0 100.6 jit_solution(15104974865383789922)
XLA Ops:
  0.6 0.0 copy-start.1
  0.6 0.0 copy-start
  0.7 1.6 %shard_map.77 = f32[64,16,128]{2,1,0:T(8,128)} custom-call(f32[2,4096]{1,0:T(2,128)} %bitcast.8), custom_call_target="tpu_custom_call" | custom-call | tf_op jit(solution)/shard_map/pallas_call | solution.py:301
  2.3 18.9 %all-to-all-start = ((f32[64,16,128]{2,1,0:T(8,128)}), f32[64,16,128]{2,1,0:T(8,128)S(1)}, u32[]{:S(2)}, u32[]{:S(2)}) async-start(f32[64,16,128]{2,1,0:T(8,128)} %shard_map.77), calls=%async_computation | async-start | bytes 1048576 | tf_op jit(solution)/shard_map/all_to_all | solution.py:317
  21.1 1.7 %shard_map.78.rows_ref = f32[264,128]{1,0:T(8,128)S(1)} custom-call(s32[256]{0:T(256)} %index_hbm, s32[2048]{0:T(1024)} %labels_hbm.1, f32[2048,128]{1,0:T(8,128)} %pool_hbm.1), custom_call_target="tpu_custom_call" | custom-call | tf_op jit(solution)/shard_map/pallas_call | solution.py:305
  22.9 3.4 %collective-permute-start.2 = (f32[264,128]{1,0:T(8,128)S(1)}, f32[264,128]{1,0:T(8,128)S(1)}, u32[]{:S(2)}, u32[]{:S(2)}) collective-permute-start(f32[264,128]{1,0:T(8,128)S(1)} %shard_map.78.rows_ref), channel_id=1, source_target_pairs={{0,8},{8,0},{64,72},{72,64},{1,9},{9,1},{65,73},{73,65},{2,10},{10... | collective-permute-start | bytes 405512 | tf_op jit(solution)/shard_map/ppermute | solution.py:318
  26.3 2.5 %collective-permute-start.1 = (f32[264,128]{1,0:T(8,128)S(1)}, f32[264,128]{1,0:T(8,128)S(1)}, u32[]{:S(2)}, u32[]{:S(2)}) collective-permute-start(f32[264,128]{1,0:T(8,128)S(1)} %shard_map.78.rows_ref), channel_id=1, source_target_pairs={{0,72},{8,64},{64,8},{72,0},{1,73},{9,65},{65,9},{73,1},{2,74},{10... | collective-permute-start | bytes 405512 | tf_op jit(solution)/shard_map/ppermute | solution.py:318
  28.8 3.3 %collective-permute-start = (f32[264,128]{1,0:T(8,128)S(1)}, f32[264,128]{1,0:T(8,128)S(1)}, u32[]{:S(2)}, u32[]{:S(2)}) collective-permute-start(f32[264,128]{1,0:T(8,128)S(1)} %shard_map.78.rows_ref), channel_id=1, source_target_pairs={{0,64},{8,72},{64,0},{72,8},{1,65},{9,73},{65,1},{73,9},{2,66},{10... | collective-permute-start | bytes 405512 | tf_op jit(solution)/shard_map/ppermute | solution.py:318
  32.1 0.0 copy-done.1
  32.2 0.0 copy-done
  32.2 0.2 shard_map.80.kinds_ref
  32.4 5.1 %collective-permute-done.2.rows1_ref = f32[264,128]{1,0:T(8,128)S(1)} collective-permute-done((f32[264,128]{1,0:T(8,128)S(1)}, f32[264,128]{1,0:T(8,128)S(1)}, u32[]{:S(2)}, u32[]{:S(2)}) %collective-permute-start.2) | collective-permute-done | bytes 135200 | tf_op jit(solution)/shard_map/ppermute | solution.py:318
  37.5 0.2 shard_map.79
  37.8 0.0 all-to-all-done
  37.8 1.8 %shard_map.81 = (f32[512,1024]{1,0:T(8,128)S(1)}, f32[8,128]{1,0:T(8,128)S(1)}, bf16[896,1024]{1,0:T(8,128)(2,1)S(1)}, f32[8,1024]{1,0:T(8,128)S(1)}) custom-call(bf16[512,896]{1,0:T(8,128)(2,1)S(1)} %get-tuple-element.21.left_ref, f32[512,128]{1,0:T(8,128)S(1)} %get-tuple-element.22.left_squares_ref, f32[1024,128]{1,0:T(8,128)S(1)} %bitcast.6, ...), custom_call_target="tpu_custom_call" | custom-call | tf_op jit(solution)/shard_map/pallas_call | solution.py:325
  39.6 0.0 collective-permute-done.1.rows3_ref
  39.7 0.0 collective-permute-done.rows2_ref
  39.7 1.7 %shard_map.82 = (f32[512,1024]{1,0:T(8,128)S(1)}, f32[32,8,128]{2,1,0:T(8,128)S(1)}) custom-call(f32[264,128]{1,0:T(8,128)S(1)} %collective-permute-done.rows2_ref, f32[264,128]{1,0:T(8,128)S(1)} %collective-permute-done.1.rows3_ref, bf16[896,1024]{1,0:T(8,128)(2,1)S(1)} %get-tuple-element.26.b_ref, f32[8,1024]{1,0:T(8,128)S(1)} %get-tuple-element.27.squares_ref, ...), custom_call_target="tpu_custom_call" | custom-call | tf_op jit(solution)/shard_map/pallas_call | solution.py:331
  41.4 10.0 %all_to_all.25.parts_ref = f32[32,8,128]{2,1,0:T(8,128)S(1)} all-to-all(f32[32,8,128]{2,1,0:T(8,128)S(1)} %get-tuple-element.29), channel_id=1, replica_groups={{77,76,79,78,73,72,75,74,69,68,71,70,65,64,67,66,13,12,15,14,9,8,11,10,..., dimensions={0} | all-to-all | bytes 262144 | tf_op jit(solution)/shard_map/all_to_all | solution.py:338
  51.4 1.0 %shard_map.83 = f32[16,8,128]{2,1,0:T(8,128)S(1)} custom-call(f32[32,8,128]{2,1,0:T(8,128)S(1)} %all_to_all.25.parts_ref, f32[512,1024]{1,0:T(8,128)S(1)} %get-tuple-element.30.first_ref, f32[512,1024]{1,0:T(8,128)S(1)} %get-tuple-element.31.rest_ref, s32[1]{0:T(128)} %bitcast.2.quarter_ref), custom_call_target="tpu_custom_call" | custom-call | tf_op jit(solution)/shard_map/pallas_call | solution.py:339
  52.4 14.7 %all_to_all.26.parts_ref = f32[16,8,128]{2,1,0:T(8,128)S(1)} all-to-all(f32[16,8,128]{2,1,0:T(8,128)S(1)} %shard_map.83), channel_id=1, replica_groups={{288,304,256,272,416,432,384,400,32,48,0,16,160,176,128,144},{289,305,2..., dimensions={0} | all-to-all | bytes 131072 | tf_op jit(solution)/shard_map/all_to_all | solution.py:340
  67.2 0.9 shard_map.84
  68.1 9.6 %all_to_all.27.parts_ref = f32[32,8,128]{2,1,0:T(8,128)S(1)} all-to-all(f32[32,8,128]{2,1,0:T(8,128)S(1)} %shard_map.84), channel_id=1, replica_groups={{77,76,79,78,73,72,75,74,69,68,71,70,65,64,67,66,13,12,15,14,9,8,11,10,..., dimensions={0} | all-to-all | bytes 262144 | tf_op jit(solution)/shard_map/all_to_all | solution.py:342
  77.6 1.1 %shard_map.85 = (f32[64,1,1152]{2,1,0:T(1,128)S(1)}, f32[8,128]{1,0:T(8,128)S(1)}) custom-call(f32[32,8,128]{2,1,0:T(8,128)S(1)} %all_to_all.27.parts_ref, f32[512,1024]{1,0:T(8,128)S(1)} %get-tuple-element.30.first_ref, f32[512,1024]{1,0:T(8,128)S(1)} %get-tuple-element.31.rest_ref, s32[1]{0:T(128)} %bitcast.2.quarter_ref), custom_call_target="tpu_custom_call" | custom-call | tf_op jit(solution)/shard_map/pallas_call | solution.py:343
  78.8 21.1 %all_to_all.28.parts_ref = f32[64,1,1152]{2,1,0:T(1,128)S(1)} all-to-all(f32[64,1,1152]{2,1,0:T(1,128)S(1)} %get-tuple-element.32), channel_id=1, replica_groups={{288,296,304,312,256,264,272,280,352,360,368,376,320,328,336,344,416,42..., dimensions={0} | all-to-all | bytes 589824 | tf_op jit(solution)/shard_map/all_to_all | solution.py:346
  99.9 0.7 shard_map.86
Async XLA Ops:
  0.6 31.5 %copy-start.1 = (f32[10,10]{1,0:T(8,128)S(1)}, f32[10,10]{1,0:T(8,128)}, u32[]{:S(2)}) copy-start(f32[10,10]{1,0:T(8,128)} %class_ref) | copy-start | bytes 1204
  0.6 31.5 %copy-start = (s32[4096]{0:T(1024)S(1)}, s32[4096]{0:T(1024)}, u32[]{:S(2)}) copy-start(s32[4096]{0:T(1024)} %param.10) | copy-start | bytes 49156
  2.3 35.5 %all-to-all-start = ((f32[64,16,128]{2,1,0:T(8,128)}), f32[64,16,128]{2,1,0:T(8,128)S(1)}, u32[]{:S(2)}, u32[]{:S(2)}) async-start(f32[64,16,128]{2,1,0:T(8,128)} %shard_map.77), calls=%async_computation | async-start | bytes 1048576 | tf_op jit(solution)/shard_map/all_to_all | solution.py:317
  22.9 14.6 %collective-permute-start.2 = (f32[264,128]{1,0:T(8,128)S(1)}, f32[264,128]{1,0:T(8,128)S(1)}, u32[]{:S(2)}, u32[]{:S(2)}) collective-permute-start(f32[264,128]{1,0:T(8,128)S(1)} %shard_map.78.rows_ref), channel_id=1, source_target_pairs={{0,8},{8,0},{64,72},{72,64},{1,9},{9,1},{65,73},{73,65},{2,10},{10... | collective-permute-start | bytes 405512 | tf_op jit(solution)/shard_map/ppermute | solution.py:318
  26.3 13.4 %collective-permute-start.1 = (f32[264,128]{1,0:T(8,128)S(1)}, f32[264,128]{1,0:T(8,128)S(1)}, u32[]{:S(2)}, u32[]{:S(2)}) collective-permute-start(f32[264,128]{1,0:T(8,128)S(1)} %shard_map.78.rows_ref), channel_id=1, source_target_pairs={{0,72},{8,64},{64,8},{72,0},{1,73},{9,65},{65,9},{73,1},{2,74},{10... | collective-permute-start | bytes 405512 | tf_op jit(solution)/shard_map/ppermute | solution.py:318
  28.8 10.8 %collective-permute-start = (f32[264,128]{1,0:T(8,128)S(1)}, f32[264,128]{1,0:T(8,128)S(1)}, u32[]{:S(2)}, u32[]{:S(2)}) collective-permute-start(f32[264,128]{1,0:T(8,128)S(1)} %shard_map.78.rows_ref), channel_id=1, source_target_pairs={{0,64},{8,72},{64,0},{72,8},{1,65},{9,73},{65,1},{73,9},{2,66},{10... | collective-permute-start | bytes 405512 | tf_op jit(solution)/shard_map/ppermute | solution.py:318

commit v7 on v6

--- a/solution.py
+++ b/solution.py
@@ -120,12 +120,13 @@
     classes = class_ref.shape[0]
     own = labels_ref[pl.ds(pl.multiple_of(quarter_ref[0] * NB, NB), NB), :]
     kinds = class_ref[...] * (-SCALE)
+    ones = jnp.where(lax.broadcasted_iota(jnp.int32, (16, T), 0) < 3, 1.0, 0.0).astype(BF16)
     for block in range(NB):
         onehot = (lax.broadcasted_iota(jnp.int32, (classes, T), 0) == own[block : block + 1]).astype(F32)
         mapped = jnp.dot(kinds, onehot, precision=lax.Precision.HIGHEST, preferred_element_type=F32)
         mapped = jnp.concatenate([mapped, jnp.zeros((16 - classes, T), F32)], axis=0)
         hi, mid, low = split3(mapped)
-        filled = jnp.concatenate([hi, mid, low, jnp.zeros((T - 48, T), BF16)], axis=0)
+        filled = jnp.concatenate([hi, mid, low, ones, jnp.zeros((T - 64, T), BF16)], axis=0)
         out_ref[:, block * T : (block + 1) * T] = filled
 
 
@@ -145,20 +146,20 @@
     lane = lax.broadcasted_iota(jnp.int32, (OWN, T), 1)
     flat = [jnp.broadcast_to(rows_ref[OWN + k : OWN + k + 1, :], (T, T)).T for k in range(OWN // T)]
     label = jnp.concatenate(flat, axis=0).astype(jnp.int32)
-    ext = jnp.where((lane % 16 == label) & (lane < 48), 1.0, 0.0).astype(BF16)
-    return jnp.concatenate([hi, hi, mid, hi, low, mid, ext], axis=1), squares
-
-
-def left_kernel(rows_ref, rows1_ref, left_ref, squares_ref):
+    ext = jnp.where((lane % 16 == label) | (lane >= 51), 1.0, 0.0)
+    for k, part in enumerate(split3(squares)):
+        ext = jnp.where(lane == 48 + k, part.astype(F32), ext)
+    ext = jnp.where(lane < 54, ext, 0.0).astype(BF16)
+    return jnp.concatenate([hi, hi, mid, hi, low, mid, ext], axis=1)
+
+
+def left_kernel(rows_ref, rows1_ref, left_ref):
     for k, ref in enumerate((rows_ref, rows1_ref)):
-        a, squares = left_rows(ref)
-        left_ref[k * OWN : (k + 1) * OWN, :] = a
-        squares_ref[k * OWN : (k + 1) * OWN, :] = jnp.broadcast_to(squares, (OWN, T))
-
-
-def group_costs(left, b, squares_v, cost_ref, start):
-    a, squares = left
-    cost_ref[start : start + OWN, :] = jnp.dot(a, b, preferred_element_type=F32) + squares + squares_v
+        left_ref[k * OWN : (k + 1) * OWN, :] = left_rows(ref)
+
+
+def group_costs(left, b, cost_ref, start):
+    cost_ref[start : start + OWN, :] = jnp.dot(left, b, preferred_element_type=F32)
 
 
 def group_lse(cost_ref, start, place, part_ref, piece_ref):
@@ -171,30 +172,35 @@
         part_ref[pl.ds(place + half, 1), :] = rows_block(load, piece_ref.at[half])
 
 
-def first_costs_kernel(left_ref, left_squares_ref, val_ref, kinds_ref, quarter_ref, cost_ref, part_ref, b_ref, squares_ref, piece_ref):
+def first_costs_kernel(left_ref, val_ref, kinds_ref, quarter_ref, cost_ref, part_ref, b_ref, piece_ref):
     for block in range(NB):
         lanes = slice(block * T, (block + 1) * T)
         y = in_order(val_ref[pl.ds(block, T, stride=NB), :])
         hi, mid, low = split3(y)
         for k, part in enumerate((hi, mid, hi, low, hi, mid)):
             b_ref[k * T : (k + 1) * T, lanes] = part
-        squares_ref[:, lanes] = jnp.broadcast_to(jnp.sum(y * y, axis=0, keepdims=True) * (-SCALE / T), (8, T))
-    b_ref[6 * T : 7 * T, :] = kinds_ref[...]
-    lefts = [(left_ref[rows, :], left_squares_ref[rows, 0:1]) for rows in (slice(0, OWN), slice(OWN, 2 * OWN))]
-    tile_costs(lefts, (0, 1), quarter_ref[0], b_ref, squares_ref, cost_ref, part_ref, piece_ref)
+        ext = kinds_ref[48:64, lanes].astype(F32)
+        sub = lax.broadcasted_iota(jnp.int32, (16, T), 0)
+        for k, part in enumerate(split3(jnp.sum(y * y, axis=0, keepdims=True) * (-SCALE / T))):
+            ext = jnp.where(sub == 3 + k, part.astype(F32), ext)
+        b_ref[6 * T : 6 * T + 48, lanes] = kinds_ref[0:48, lanes]
+        b_ref[6 * T + 48 : 6 * T + 64, lanes] = ext.astype(BF16)
+        b_ref[6 * T + 64 : 7 * T, lanes] = kinds_ref[64:T, lanes]
+    lefts = [left_ref[rows, :] for rows in (slice(0, OWN), slice(OWN, 2 * OWN))]
+    tile_costs(lefts, (0, 1), quarter_ref[0], b_ref, cost_ref, part_ref, piece_ref)
 
 
 def other_costs_kernel(
-    rows2_ref, rows3_ref, b_ref, squares_ref, quarter_ref, part_ref, cost_ref, out_ref, full_ref, piece_ref
+    rows2_ref, rows3_ref, b_ref, quarter_ref, part_ref, cost_ref, out_ref, full_ref, piece_ref
 ):
     full_ref[...] = part_ref[...]
-    tile_costs((left_rows(rows2_ref), left_rows(rows3_ref)), (2, 3), quarter_ref[0], b_ref, squares_ref, cost_ref, full_ref, piece_ref)
+    tile_costs((left_rows(rows2_ref), left_rows(rows3_ref)), (2, 3), quarter_ref[0], b_ref, cost_ref, full_ref, piece_ref)
     send(full_ref, out_ref)
 
 
-def tile_costs(lefts, aparts, quarter, b_ref, squares_ref, cost_ref, part_ref, piece_ref):
+def tile_costs(lefts, aparts, quarter, b_ref, cost_ref, part_ref, piece_ref):
     for k, left in enumerate(lefts):
-        group_costs(left, b_ref[...], squares_ref[0:1, :], cost_ref, k * OWN)
+        group_costs(left, b_ref[...], cost_ref, k * OWN)
     for k, apart in enumerate(aparts):
         group_lse(cost_ref, k * OWN, (quarter ^ apart) * 2, part_ref, piece_ref.at[k])
 
@@ -321,19 +327,19 @@
         quarter, val_labels.reshape(32, T), class_cost
     )
     part, piece, wide = vmem((NB, T)), vmem((NB, T, T)), vmem((SIDE, T))
-    left, left_squares = call(left_kernel, [shape((2 * OWN, 7 * T), BF16), shape((2 * OWN, T))], [SPEC] * 2)(rows, others[1])
-    first, part_first, b, squares = call(
+    (left,) = call(left_kernel, [shape((2 * OWN, 7 * T), BF16)], [SPEC] * 2)(rows, others[1])
+    first, part_first, b = call(
         first_costs_kernel,
-        [shape((2 * OWN, SIDE)), shape((NB, T)), shape((7 * T, SIDE), BF16), shape((8, SIDE))],
-        [SPEC] * 4 + [SCALARS],
+        [shape((2 * OWN, SIDE)), shape((NB, T)), shape((7 * T, SIDE), BF16)],
+        [SPEC] * 3 + [SCALARS],
         [vmem((2, 2, T, T))],
-    )(left, left_squares, columns.reshape(SIDE, T), kinds, quarter)
+    )(left, columns.reshape(SIDE, T), kinds, quarter)
     rest, parts = call(
         other_costs_kernel,
         [shape((2 * OWN, SIDE)), shape((32, NB, T))],
-        [SPEC] * 4 + [SCALARS, SPEC],
+        [SPEC] * 3 + [SCALARS, SPEC],
         [part, vmem((2, 2, T, T))],
-    )(others[2], others[3], b, squares, quarter, part_first)
+    )(others[2], others[3], b, quarter, part_first)
     step = [SPEC] * 3 + [SCALARS]
     parts = lax.all_to_all(parts, ALONG, 0, 0, axis_index_groups=ALONG_ORDER)
     (parts,) = call(columns_step_kernel, [shape((16, NB, T))], step, [wide, part, part])(parts, first, rest, quarter)

time: 101 us -> 101 us (level)
  transfers between devices with their start and end apart: 4 -> 4, of which waited for: 1 -> 2; matrix products, arithmetic and copies ran while one was open for 0% -> 0% of each run, Pallas kernels for 4% -> 4%
where the time goes in v7:
time: 101 us
  blocking collectives  55.5 us (55%)
  starting transfers between devices  28.1 us (28%)
  Pallas kernels  11 us (11%)
  waiting for transfers between devices  5.19 us (5%)
    all_to_all x1, blocking collectives, local(): parts = lax.all_to_all(parts, ROW, 0, 0, axis_index_groups=ROW_ORDER)  21.1 us
    all_to_all x2, blocking collectives, local(): parts = lax.all_to_all(parts, ALONG, 0, 0, axis_index_groups=ALONG_ORDER)  19.6 us
    all_to_all x1, starting transfers between devices, local(): columns = lax.all_to_all(columns, ROW, 0, 0, axis_index_groups=ROW_ORDER)  18.9 us
    all_to_all x1, blocking collectives, local(): parts = lax.all_to_all(parts, ACROSS, 0, 0, axis_index_groups=ACROSS_ORDER)  14.7 us
    ppermute x3, starting transfers between devices, local(): lax.ppermute(rows, QUAD, [(i, i ^ apart) for i in range(4)])  9.21 us
    ppermute x3, waiting for transfers between devices, local(): lax.ppermute(rows, QUAD, [(i, i ^ apart) for i in range(4)])  5.19 us
  transfers between devices with their start and end apart: 4, of which 2 were waited for; matrix products, arithmetic and copies ran while one was open for 0% of the time, Pallas kernels for 4%

profile of v7, /device:TPU:8, one launch (start us, length us, event | category | flops | bytes accessed | tf_op | source)
XLA Modules:
  0.0 100.5 jit_solution(10518947662209616222)
XLA Ops:
  0.6 0.0 copy-start.1
  0.6 0.0 copy-start
  0.7 1.6 %shard_map.77 = f32[64,16,128]{2,1,0:T(8,128)} custom-call(f32[2,4096]{1,0:T(2,128)} %bitcast.8), custom_call_target="tpu_custom_call" | custom-call | tf_op jit(solution)/shard_map/pallas_call | solution.py:307
  2.3 18.9 %all-to-all-start = ((f32[64,16,128]{2,1,0:T(8,128)}), f32[64,16,128]{2,1,0:T(8,128)S(1)}, u32[]{:S(2)}, u32[]{:S(2)}) async-start(f32[64,16,128]{2,1,0:T(8,128)} %shard_map.77), calls=%async_computation | async-start | bytes 1048576 | tf_op jit(solution)/shard_map/all_to_all | solution.py:323
  21.2 1.7 %shard_map.78.rows_ref = f32[264,128]{1,0:T(8,128)S(1)} custom-call(s32[256]{0:T(256)} %index_hbm, s32[2048]{0:T(1024)} %labels_hbm.1, f32[2048,128]{1,0:T(8,128)} %pool_hbm.1), custom_call_target="tpu_custom_call" | custom-call | tf_op jit(solution)/shard_map/pallas_call | solution.py:311
  22.9 3.4 %collective-permute-start.2 = (f32[264,128]{1,0:T(8,128)S(1)}, f32[264,128]{1,0:T(8,128)S(1)}, u32[]{:S(2)}, u32[]{:S(2)}) collective-permute-start(f32[264,128]{1,0:T(8,128)S(1)} %shard_map.78.rows_ref), channel_id=1, source_target_pairs={{0,8},{8,0},{64,72},{72,64},{1,9},{9,1},{65,73},{73,65},{2,10},{10... | collective-permute-start | bytes 405512 | tf_op jit(solution)/shard_map/ppermute | solution.py:324
  26.3 2.5 %collective-permute-start.1 = (f32[264,128]{1,0:T(8,128)S(1)}, f32[264,128]{1,0:T(8,128)S(1)}, u32[]{:S(2)}, u32[]{:S(2)}) collective-permute-start(f32[264,128]{1,0:T(8,128)S(1)} %shard_map.78.rows_ref), channel_id=1, source_target_pairs={{0,72},{8,64},{64,8},{72,0},{1,73},{9,65},{65,9},{73,1},{2,74},{10... | collective-permute-start | bytes 405512 | tf_op jit(solution)/shard_map/ppermute | solution.py:324
  28.8 3.3 %collective-permute-start = (f32[264,128]{1,0:T(8,128)S(1)}, f32[264,128]{1,0:T(8,128)S(1)}, u32[]{:S(2)}, u32[]{:S(2)}) collective-permute-start(f32[264,128]{1,0:T(8,128)S(1)} %shard_map.78.rows_ref), channel_id=1, source_target_pairs={{0,64},{8,72},{64,0},{72,8},{1,65},{9,73},{65,1},{73,9},{2,66},{10... | collective-permute-start | bytes 405512 | tf_op jit(solution)/shard_map/ppermute | solution.py:324
  32.2 0.0 copy-done.1
  32.2 0.0 copy-done
  32.2 0.2 shard_map.80.kinds_ref
  32.4 5.1 %collective-permute-done.2.rows1_ref = f32[264,128]{1,0:T(8,128)S(1)} collective-permute-done((f32[264,128]{1,0:T(8,128)S(1)}, f32[264,128]{1,0:T(8,128)S(1)}, u32[]{:S(2)}, u32[]{:S(2)}) %collective-permute-start.2) | collective-permute-done | bytes 135200 | tf_op jit(solution)/shard_map/ppermute | solution.py:324
  37.5 0.3 shard_map.79.left_ref
  37.8 0.0 all-to-all-done
  37.8 1.8 %shard_map.81 = (f32[512,1024]{1,0:T(8,128)S(1)}, f32[8,128]{1,0:T(8,128)S(1)}, bf16[896,1024]{1,0:T(8,128)(2,1)S(1)}) custom-call(bf16[512,896]{1,0:T(8,128)(2,1)S(1)} %shard_map.79.left_ref, f32[1024,128]{1,0:T(8,128)S(1)} %bitcast.6, bf16[128,1024]{1,0:T(8,128)(2,1)S(1)} %shard_map.80.kinds_ref, s32[1]{0:T(128)} %bitcast.2.quarter_ref), custom_call_target="tpu_custom_call" | custom-call | tf_op jit(solution)/shard_map/pallas_call | solution.py:331
  39.6 0.1 collective-permute-done.1.rows3_ref
  39.7 0.0 collective-permute-done.rows2_ref
  39.7 1.6 %shard_map.82 = (f32[512,1024]{1,0:T(8,128)S(1)}, f32[32,8,128]{2,1,0:T(8,128)S(1)}) custom-call(f32[264,128]{1,0:T(8,128)S(1)} %collective-permute-done.rows2_ref, f32[264,128]{1,0:T(8,128)S(1)} %collective-permute-done.1.rows3_ref, bf16[896,1024]{1,0:T(8,128)(2,1)S(1)} %get-tuple-element.21.b_ref, s32[1]{0:T(128)} %bitcast.2.quarter_ref, ...), custom_call_target="tpu_custom_call" | custom-call | tf_op jit(solution)/shard_map/pallas_call | solution.py:337
  41.3 10.1 %all_to_all.25.parts_ref = f32[32,8,128]{2,1,0:T(8,128)S(1)} all-to-all(f32[32,8,128]{2,1,0:T(8,128)S(1)} %get-tuple-element.23), channel_id=1, replica_groups={{77,76,79,78,73,72,75,74,69,68,71,70,65,64,67,66,13,12,15,14,9,8,11,10,..., dimensions={0} | all-to-all | bytes 262144 | tf_op jit(solution)/shard_map/all_to_all | solution.py:344
  51.3 1.0 %shard_map.83 = f32[16,8,128]{2,1,0:T(8,128)S(1)} custom-call(f32[32,8,128]{2,1,0:T(8,128)S(1)} %all_to_all.25.parts_ref, f32[512,1024]{1,0:T(8,128)S(1)} %get-tuple-element.24.first_ref, f32[512,1024]{1,0:T(8,128)S(1)} %get-tuple-element.25.rest_ref, s32[1]{0:T(128)} %bitcast.2.quarter_ref), custom_call_target="tpu_custom_call" | custom-call | tf_op jit(solution)/shard_map/pallas_call | solution.py:345
  52.4 14.7 %all_to_all.26.parts_ref = f32[16,8,128]{2,1,0:T(8,128)S(1)} all-to-all(f32[16,8,128]{2,1,0:T(8,128)S(1)} %shard_map.83), channel_id=1, replica_groups={{288,304,256,272,416,432,384,400,32,48,0,16,160,176,128,144},{289,305,2..., dimensions={0} | all-to-all | bytes 131072 | tf_op jit(solution)/shard_map/all_to_all | solution.py:346
  67.1 0.9 shard_map.84
  68.0 9.6 %all_to_all.27.parts_ref = f32[32,8,128]{2,1,0:T(8,128)S(1)} all-to-all(f32[32,8,128]{2,1,0:T(8,128)S(1)} %shard_map.84), channel_id=1, replica_groups={{77,76,79,78,73,72,75,74,69,68,71,70,65,64,67,66,13,12,15,14,9,8,11,10,..., dimensions={0} | all-to-all | bytes 262144 | tf_op jit(solution)/shard_map/all_to_all | solution.py:348
  77.5 1.1 %shard_map.85 = (f32[64,1,1152]{2,1,0:T(1,128)S(1)}, f32[8,128]{1,0:T(8,128)S(1)}) custom-call(f32[32,8,128]{2,1,0:T(8,128)S(1)} %all_to_all.27.parts_ref, f32[512,1024]{1,0:T(8,128)S(1)} %get-tuple-element.24.first_ref, f32[512,1024]{1,0:T(8,128)S(1)} %get-tuple-element.25.rest_ref, s32[1]{0:T(128)} %bitcast.2.quarter_ref), custom_call_target="tpu_custom_call" | custom-call | tf_op jit(solution)/shard_map/pallas_call | solution.py:349
  78.7 21.1 %all_to_all.28.parts_ref = f32[64,1,1152]{2,1,0:T(1,128)S(1)} all-to-all(f32[64,1,1152]{2,1,0:T(1,128)S(1)} %get-tuple-element.26), channel_id=1, replica_groups={{288,296,304,312,256,264,272,280,352,360,368,376,320,328,336,344,416,42..., dimensions={0} | all-to-all | bytes 589824 | tf_op jit(solution)/shard_map/all_to_all | solution.py:352
  99.8 0.7 shard_map.86
Async XLA Ops:
  0.6 31.5 %copy-start.1 = (f32[10,10]{1,0:T(8,128)S(1)}, f32[10,10]{1,0:T(8,128)}, u32[]{:S(2)}) copy-start(f32[10,10]{1,0:T(8,128)} %class_ref) | copy-start | bytes 1204
  0.6 31.5 %copy-start = (s32[4096]{0:T(1024)S(1)}, s32[4096]{0:T(1024)}, u32[]{:S(2)}) copy-start(s32[4096]{0:T(1024)} %param.10) | copy-start | bytes 49156
  2.3 35.5 %all-to-all-start = ((f32[64,16,128]{2,1,0:T(8,128)}), f32[64,16,128]{2,1,0:T(8,128)S(1)}, u32[]{:S(2)}, u32[]{:S(2)}) async-start(f32[64,16,128]{2,1,0:T(8,128)} %shard_map.77), calls=%async_computation | async-start | bytes 1048576 | tf_op jit(solution)/shard_map/all_to_all | solution.py:323
  22.9 14.6 %collective-permute-start.2 = (f32[264,128]{1,0:T(8,128)S(1)}, f32[264,128]{1,0:T(8,128)S(1)}, u32[]{:S(2)}, u32[]{:S(2)}) collective-permute-start(f32[264,128]{1,0:T(8,128)S(1)} %shard_map.78.rows_ref), channel_id=1, source_target_pairs={{0,8},{8,0},{64,72},{72,64},{1,9},{9,1},{65,73},{73,65},{2,10},{10... | collective-permute-start | bytes 405512 | tf_op jit(solution)/shard_map/ppermute | solution.py:324
  26.3 13.4 %collective-permute-start.1 = (f32[264,128]{1,0:T(8,128)S(1)}, f32[264,128]{1,0:T(8,128)S(1)}, u32[]{:S(2)}, u32[]{:S(2)}) collective-permute-start(f32[264,128]{1,0:T(8,128)S(1)} %shard_map.78.rows_ref), channel_id=1, source_target_pairs={{0,72},{8,64},{64,8},{72,0},{1,73},{9,65},{65,9},{73,1},{2,74},{10... | collective-permute-start | bytes 405512 | tf_op jit(solution)/shard_map/ppermute | solution.py:324
  28.8 10.8 %collective-permute-start = (f32[264,128]{1,0:T(8,128)S(1)}, f32[264,128]{1,0:T(8,128)S(1)}, u32[]{:S(2)}, u32[]{:S(2)}) collective-permute-start(f32[264,128]{1,0:T(8,128)S(1)} %shard_map.78.rows_ref), channel_id=1, source_target_pairs={{0,64},{8,72},{64,0},{72,8},{1,65},{9,73},{65,1},{73,9},{2,66},{10... | collective-permute-start | bytes 405512 | tf_op jit(solution)/shard_map/ppermute | solution.py:324

commit v8 on v5

--- a/solution.py
+++ b/solution.py
@@ -173,14 +173,14 @@
             b_ref[k * T : (k + 1) * T, lanes] = part
         squares_ref[:, lanes] = jnp.broadcast_to(jnp.sum(y * y, axis=0, keepdims=True) * (-SCALE / T), (8, T))
     b_ref[6 * T : 7 * T, :] = kinds_ref[...]
-    tile_costs((rows_ref, rows3_ref), (0, 3), quarter_ref[0], b_ref, squares_ref, cost_ref, part_ref, piece_ref)
+    tile_costs((rows_ref, rows3_ref), (0, 1), quarter_ref[0], b_ref, squares_ref, cost_ref, part_ref, piece_ref)
 
 
 def other_costs_kernel(
     rows1_ref, rows2_ref, b_ref, squares_ref, quarter_ref, part_ref, cost_ref, out_ref, full_ref, piece_ref
 ):
     full_ref[...] = part_ref[...]
-    tile_costs((rows1_ref, rows2_ref), (1, 2), quarter_ref[0], b_ref, squares_ref, cost_ref, full_ref, piece_ref)
+    tile_costs((rows1_ref, rows2_ref), (2, 3), quarter_ref[0], b_ref, squares_ref, cost_ref, full_ref, piece_ref)
     send(full_ref, out_ref)
 
 
@@ -196,7 +196,7 @@
 
 
 def place(quarter, s):
-    return (quarter ^ (0, 3, 1, 2)[s // 2]) * 2 + s % 2
+    return (quarter ^ (0, 1, 2, 3)[s // 2]) * 2 + s % 2
 
 
 def rows_step_kernel(parts_ref, first_ref, rest_ref, quarter_ref, out_ref, piece_ref, part_ref):
@@ -307,7 +307,7 @@
         ],
     )(far(window_index), far(pool_labels), far(pool))
     columns = lax.all_to_all(columns, ROW, 0, 0, axis_index_groups=ROW_ORDER)
-    others = [lax.ppermute(rows, QUAD, [(i, i ^ apart) for i in range(4)]) for apart in (1, 2, 3)]
+    others = {apart: lax.ppermute(rows, QUAD, [(i, i ^ apart) for i in range(4)]) for apart in (2, 3, 1)}
     rows, val_labels, class_cost = lax.optimization_barrier((rows, val_labels, class_cost))
     (kinds,) = call(labels_kernel, [shape((T, SIDE), BF16)], [SCALARS, SPEC, SPEC])(
         quarter, val_labels.reshape(32, T), class_cost
@@ -318,13 +318,13 @@
         [shape((2 * OWN, SIDE)), shape((NB, T)), shape((7 * T, SIDE), BF16), shape((8, SIDE))],
         [SPEC] * 4 + [SCALARS],
         [vmem((2, 2, T, T))],
-    )(rows, others[2], columns.reshape(SIDE, T), kinds, quarter)
+    )(rows, others[1], columns.reshape(SIDE, T), kinds, quarter)
     rest, parts = call(
         other_costs_kernel,
         [shape((2 * OWN, SIDE)), shape((32, NB, T))],
         [SPEC] * 4 + [SCALARS, SPEC],
         [part, vmem((2, 2, T, T))],
-    )(*others[:2], b, squares, quarter, part_first)
+    )(others[2], others[3], b, squares, quarter, part_first)
     step = [SPEC] * 3 + [SCALARS]
     parts = lax.all_to_all(parts, ALONG, 0, 0, axis_index_groups=ALONG_ORDER)
     (parts,) = call(columns_step_kernel, [shape((16, NB, T))], step, [wide, part, part])(parts, first, rest, quarter)

time: 101 us -> 101 us (level)
  transfers between devices with their start and end apart: 4 -> 4, of which waited for: 1 -> 2; matrix products, arithmetic and copies ran while one was open for 0% -> 0% of each run, Pallas kernels for 4% -> 4%
where the time goes in v8:
time: 101 us; the launch traced here: 100 us
  blocking collectives  55.5 us (55%)
  starting transfers between devices  28.1 us (28%)
  Pallas kernels  10.7 us (11%)
  waiting for transfers between devices  5.36 us (5%)
    all_to_all x1, blocking collectives, local(): parts = lax.all_to_all(parts, ROW, 0, 0, axis_index_groups=ROW_ORDER)  21.1 us
    all_to_all x2, blocking collectives, local(): parts = lax.all_to_all(parts, ALONG, 0, 0, axis_index_groups=ALONG_ORDER)  19.6 us
    all_to_all x1, starting transfers between devices, local(): columns = lax.all_to_all(columns, ROW, 0, 0, axis_index_groups=ROW_ORDER)  18.9 us
    all_to_all x1, blocking collectives, local(): parts = lax.all_to_all(parts, ACROSS, 0, 0, axis_index_groups=ACROSS_ORDER)  14.7 us
    ppermute x3, starting transfers between devices, local(): lax.ppermute(rows, QUAD, [(i, i ^ apart) for i in range(4)])  9.21 us
    ppermute x3, waiting for transfers between devices, local(): lax.ppermute(rows, QUAD, [(i, i ^ apart) for i in range(4)])  5.35 us
  transfers between devices with their start and end apart: 4, of which 2 were waited for; matrix products, arithmetic and copies ran while one was open for 0% of the time, Pallas kernels for 4%

profile of v8, /device:TPU:8, one launch (start us, length us, event | category | flops | bytes accessed | tf_op | source)
XLA Modules:
  0.0 100.4 jit_solution(12212252699760220712)
XLA Ops:
  0.6 0.0 copy-start.1
  0.6 0.0 copy-start
  0.7 1.6 %shard_map.77 = f32[64,16,128]{2,1,0:T(8,128)} custom-call(f32[2,4096]{1,0:T(2,128)} %bitcast.8), custom_call_target="tpu_custom_call" | custom-call | tf_op jit(solution)/shard_map/pallas_call | solution.py:293
  2.3 18.9 %all-to-all-start = ((f32[64,16,128]{2,1,0:T(8,128)}), f32[64,16,128]{2,1,0:T(8,128)S(1)}, u32[]{:S(2)}, u32[]{:S(2)}) async-start(f32[64,16,128]{2,1,0:T(8,128)} %shard_map.77), calls=%async_computation | async-start | bytes 1048576 | tf_op jit(solution)/shard_map/all_to_all | solution.py:309
  21.2 1.7 %shard_map.78.rows_ref = f32[264,128]{1,0:T(8,128)S(1)} custom-call(s32[256]{0:T(256)} %index_hbm, s32[2048]{0:T(1024)} %labels_hbm.1, f32[2048,128]{1,0:T(8,128)} %pool_hbm.1), custom_call_target="tpu_custom_call" | custom-call | tf_op jit(solution)/shard_map/pallas_call | solution.py:297
  22.9 3.4 %collective-permute-start.2 = (f32[264,128]{1,0:T(8,128)S(1)}, f32[264,128]{1,0:T(8,128)S(1)}, u32[]{:S(2)}, u32[]{:S(2)}) collective-permute-start(f32[264,128]{1,0:T(8,128)S(1)} %shard_map.78.rows_ref), channel_id=1, source_target_pairs={{0,8},{8,0},{64,72},{72,64},{1,9},{9,1},{65,73},{73,65},{2,10},{10... | collective-permute-start | bytes 405512 | tf_op jit(solution)/shard_map/ppermute | solution.py:310
  26.3 2.5 %collective-permute-start.1 = (f32[264,128]{1,0:T(8,128)S(1)}, f32[264,128]{1,0:T(8,128)S(1)}, u32[]{:S(2)}, u32[]{:S(2)}) collective-permute-start(f32[264,128]{1,0:T(8,128)S(1)} %shard_map.78.rows_ref), channel_id=1, source_target_pairs={{0,72},{8,64},{64,8},{72,0},{1,73},{9,65},{65,9},{73,1},{2,74},{10... | collective-permute-start | bytes 405512 | tf_op jit(solution)/shard_map/ppermute | solution.py:310
  28.8 3.3 %collective-permute-start = (f32[264,128]{1,0:T(8,128)S(1)}, f32[264,128]{1,0:T(8,128)S(1)}, u32[]{:S(2)}, u32[]{:S(2)}) collective-permute-start(f32[264,128]{1,0:T(8,128)S(1)} %shard_map.78.rows_ref), channel_id=1, source_target_pairs={{0,64},{8,72},{64,0},{72,8},{1,65},{9,73},{65,1},{73,9},{2,66},{10... | collective-permute-start | bytes 405512 | tf_op jit(solution)/shard_map/ppermute | solution.py:310
  32.2 0.0 copy-done.1
  32.2 0.0 copy-done
  32.2 0.2 shard_map.79.kinds_ref
  32.4 5.1 %collective-permute-done.2.rows3_ref = f32[264,128]{1,0:T(8,128)S(1)} collective-permute-done((f32[264,128]{1,0:T(8,128)S(1)}, f32[264,128]{1,0:T(8,128)S(1)}, u32[]{:S(2)}, u32[]{:S(2)}) %collective-permute-start.2) | collective-permute-done | bytes 135200 | tf_op jit(solution)/shard_map/ppermute | solution.py:310
  37.5 0.0 all-to-all-done
  37.5 1.9 %shard_map.80 = (f32[512,1024]{1,0:T(8,128)S(1)}, f32[8,128]{1,0:T(8,128)S(1)}, bf16[896,1024]{1,0:T(8,128)(2,1)S(1)}, f32[8,1024]{1,0:T(8,128)S(1)}) custom-call(f32[264,128]{1,0:T(8,128)S(1)} %shard_map.78.rows_ref, f32[264,128]{1,0:T(8,128)S(1)} %collective-permute-done.2.rows3_ref, f32[1024,128]{1,0:T(8,128)S(1)} %bitcast.6, ...), custom_call_target="tpu_custom_call" | custom-call | tf_op jit(solution)/shard_map/pallas_call | solution.py:316
  39.4 0.2 collective-permute-done.1.rows2_ref
  39.7 0.0 collective-permute-done.rows1_ref
  39.7 1.7 %shard_map.81 = (f32[512,1024]{1,0:T(8,128)S(1)}, f32[32,8,128]{2,1,0:T(8,128)S(1)}) custom-call(f32[264,128]{1,0:T(8,128)S(1)} %collective-permute-done.rows1_ref, f32[264,128]{1,0:T(8,128)S(1)} %collective-permute-done.1.rows2_ref, bf16[896,1024]{1,0:T(8,128)(2,1)S(1)} %get-tuple-element.22.b_ref, f32[8,1024]{1,0:T(8,128)S(1)} %get-tuple-element.23.squares_ref, ...), custom_call_target="tpu_custom_call" | custom-call | tf_op jit(solution)/shard_map/pallas_call | solution.py:322
  41.3 10.0 %all_to_all.25.parts_ref = f32[32,8,128]{2,1,0:T(8,128)S(1)} all-to-all(f32[32,8,128]{2,1,0:T(8,128)S(1)} %get-tuple-element.25), channel_id=1, replica_groups={{77,76,79,78,73,72,75,74,69,68,71,70,65,64,67,66,13,12,15,14,9,8,11,10,..., dimensions={0} | all-to-all | bytes 262144 | tf_op jit(solution)/shard_map/all_to_all | solution.py:329
  51.4 1.0 shard_map.82
  52.4 14.7 %all_to_all.26.parts_ref = f32[16,8,128]{2,1,0:T(8,128)S(1)} all-to-all(f32[16,8,128]{2,1,0:T(8,128)S(1)} %shard_map.82), channel_id=1, replica_groups={{288,304,256,272,416,432,384,400,32,48,0,16,160,176,128,144},{289,305,2..., dimensions={0} | all-to-all | bytes 131072 | tf_op jit(solution)/shard_map/all_to_all | solution.py:331
  67.1 0.9 shard_map.83
  68.0 9.6 %all_to_all.27.parts_ref = f32[32,8,128]{2,1,0:T(8,128)S(1)} all-to-all(f32[32,8,128]{2,1,0:T(8,128)S(1)} %shard_map.83), channel_id=1, replica_groups={{77,76,79,78,73,72,75,74,69,68,71,70,65,64,67,66,13,12,15,14,9,8,11,10,..., dimensions={0} | all-to-all | bytes 262144 | tf_op jit(solution)/shard_map/all_to_all | solution.py:333
  77.6 1.0 %shard_map.84 = (f32[64,1,1152]{2,1,0:T(1,128)S(1)}, f32[8,128]{1,0:T(8,128)S(1)}) custom-call(f32[32,8,128]{2,1,0:T(8,128)S(1)} %all_to_all.27.parts_ref, f32[512,1024]{1,0:T(8,128)S(1)} %get-tuple-element.26.first_ref, f32[512,1024]{1,0:T(8,128)S(1)} %get-tuple-element.27.rest_ref, s32[1]{0:T(128)} %bitcast.2.quarter_ref), custom_call_target="tpu_custom_call" | custom-call | tf_op jit(solution)/shard_map/pallas_call | solution.py:334
  78.6 21.1 %all_to_all.28.parts_ref = f32[64,1,1152]{2,1,0:T(1,128)S(1)} all-to-all(f32[64,1,1152]{2,1,0:T(1,128)S(1)} %get-tuple-element.28), channel_id=1, replica_groups={{288,296,304,312,256,264,272,280,352,360,368,376,320,328,336,344,416,42..., dimensions={0} | all-to-all | bytes 589824 | tf_op jit(solution)/shard_map/all_to_all | solution.py:337
  99.7 0.7 shard_map.85
Async XLA Ops:
  0.6 31.5 %copy-start.1 = (f32[10,10]{1,0:T(8,128)S(1)}, f32[10,10]{1,0:T(8,128)}, u32[]{:S(2)}) copy-start(f32[10,10]{1,0:T(8,128)} %class_ref) | copy-start | bytes 1204
  0.6 31.5 %copy-start = (s32[4096]{0:T(1024)S(1)}, s32[4096]{0:T(1024)}, u32[]{:S(2)}) copy-start(s32[4096]{0:T(1024)} %param.10) | copy-start | bytes 49156
  2.3 35.2 %all-to-all-start = ((f32[64,16,128]{2,1,0:T(8,128)}), f32[64,16,128]{2,1,0:T(8,128)S(1)}, u32[]{:S(2)}, u32[]{:S(2)}) async-start(f32[64,16,128]{2,1,0:T(8,128)} %shard_map.77), calls=%async_computation | async-start | bytes 1048576 | tf_op jit(solution)/shard_map/all_to_all | solution.py:309
  22.9 14.6 %collective-permute-start.2 = (f32[264,128]{1,0:T(8,128)S(1)}, f32[264,128]{1,0:T(8,128)S(1)}, u32[]{:S(2)}, u32[]{:S(2)}) collective-permute-start(f32[264,128]{1,0:T(8,128)S(1)} %shard_map.78.rows_ref), channel_id=1, source_target_pairs={{0,8},{8,0},{64,72},{72,64},{1,9},{9,1},{65,73},{73,65},{2,10},{10... | collective-permute-start | bytes 405512 | tf_op jit(solution)/shard_map/ppermute | solution.py:310
  26.3 13.4 %collective-permute-start.1 = (f32[264,128]{1,0:T(8,128)S(1)}, f32[264,128]{1,0:T(8,128)S(1)}, u32[]{:S(2)}, u32[]{:S(2)}) collective-permute-start(f32[264,128]{1,0:T(8,128)S(1)} %shard_map.78.rows_ref), channel_id=1, source_target_pairs={{0,72},{8,64},{64,8},{72,0},{1,73},{9,65},{65,9},{73,1},{2,74},{10... | collective-permute-start | bytes 405512 | tf_op jit(solution)/shard_map/ppermute | solution.py:310
  28.8 10.8 %collective-permute-start = (f32[264,128]{1,0:T(8,128)S(1)}, f32[264,128]{1,0:T(8,128)S(1)}, u32[]{:S(2)}, u32[]{:S(2)}) collective-permute-start(f32[264,128]{1,0:T(8,128)S(1)} %shard_map.78.rows_ref), channel_id=1, source_target_pairs={{0,64},{8,72},{64,0},{72,8},{1,65},{9,73},{65,1},{73,9},{2,66},{10... | collective-permute-start | bytes 405512 | tf_op jit(solution)/shard_map/ppermute | solution.py:310
